TPU v7x, 256 devices: a whole 4x4x8 slice. The times are simulated.
256 devices in a mesh: ax: 16 (over z, core), az: 16 (over y, x).
Axes of the slice: x: 4, y: 4, z: 8, core: 2. Of those that a mesh axis runs over, the one named last changes fastest.
Arguments:
- gas_init: float32 [256, 512, 128], P('ax', 'az'), may hold values from -6 to 6
- transport: bfloat16 [3, 256, 512, 128], P(None, 'ax', 'az'), may hold values from -0.5 to 0.5, as said below
- heat_coef: float32 [256, 512], P('ax', 'az'), may hold values from 0.15 to 2.8
- bed_mask: int32 [256, 512], P('ax', 'az'), may hold values from 0 to 1, as said below
- wall_init: float32 [256, 48, 512], P(('ax', 'az')), may hold values from -6 to 6
- interface_init: float32 [256, 512], P(('ax', 'az')), may hold values from -6 to 6
- inverse_blocks: float32 [512, 48, 48], replicated, may hold values from -0.9 to 0.9, as said below
- rotation: int32 [1], replicated, may hold values from 1 to 511
Outputs:
- gas_temp: float32 [256, 512, 128], P('ax', 'az')
- wall_temp: float32 [256, 48, 512], P(('ax', 'az'))
- interface: float32 [256, 512], P(('ax', 'az'))
Inputs may be any that keep to these rules, and one draw needn't show every extreme that they name: `transport`: components 0 and 1 are Courant numbers between 0.12 and 0.3; component 2 is a heat source of one sweep. `bed_mask`: in each axial row the cells with 1 form one arc of azimuth. `inverse_blocks`: block k acts on the wall layers of Hartley mode k of the azimuth.
All inputs are finite; a program needn't handle non-finite values.
Results may differ from a plain program's by a relative error of at most 0.0003.
Values may be sent and summed in bfloat16 or wider, within the bound.
A program may use at most 128 MiB of HBM per device.

v0:
```python
import functools

import jax
import jax.numpy as jnp
import ml_dtypes
import numpy as np
from jax import lax
from jax.experimental import pallas as pl
from jax.experimental.pallas import tpu as pltpu
from jax.sharding import PartitionSpec as P

DIFFUSE = 0.04
RADIAL = 0.06
BED_COEF = 0.8
FIRST_RELAX = 0.5
TINY = 1e-06
MESH = pl.DeviceIdType.MESH
F32 = jnp.float32
BF16 = jnp.bfloat16
SECTOR = 32
TOP = 8
FIELDS = (
    [(0, r) for r in (124, 125, 126, 127)]
    + [(1, r) for r in (124, 125, 126, 127)]
    + [(0, r) for r in (125, 126, 127)]
    + [(1, r) for r in (125, 126, 127)]
    + [(2, 125), (3, 125)]
    + [(2, 127), (3, 127), (4, 127), (2, 126), (3, 126), (4, 126), (4, 125), None]
    + [(2, 127), (3, 127), (4, 127), None, None, None, None, None]
)
NFIELD = len(FIELDS)
WINDOWS = (-3, 0, -2, 0)


def hartley_parts(length):
    positions = np.arange(length, dtype=np.int64)
    phases = 2.0 * np.pi / length * ((positions[:, None] * positions[None, :]) % length)
    table = ((np.cos(phases) + np.sin(phases)) / np.sqrt(length)).astype(np.float32)
    high = table.astype(ml_dtypes.bfloat16)
    low = (table - high.astype(np.float32)).astype(ml_dtypes.bfloat16)
    return high, low


def selector():
    table = np.zeros((NFIELD, 5 * 128), np.float32)
    for row, field in enumerate(FIELDS):
        if field is not None:
            table[row, field[0] * 128 + field[1]] = 1.0
    return table.astype(ml_dtypes.bfloat16)


def split(value):
    high = value.astype(BF16)
    return high, (value - high.astype(F32)).astype(BF16)


def roll_lanes(value, amount):
    return pltpu.roll(value, amount % value.shape[1], 1)


def kernel(
    nax, naz,
    gas_hbm, tr_hbm, heat_hbm, bed_hbm, wall_hbm, th_hbm, inv_hbm, rot_ref, hh_hbm, hl_hbm, sel_hbm,
    gas_out, wall_out, th_out,
    pad, tr, heat, bed, wall, th, inv, hh, hl, sel,
    msg, recv, recv_nb, fields, tht, thn, edge, ebuf, col_out, col_in, blend, wall_res, gas_res, redsrc, redbuf,
    load_sem, out_sem, bar_unused, msg_sem, nb_sem, th_sem, edge_sem, halo_ss, halo_rs, red_sem,
):
    ax, az = lax.axis_index("ax"), lax.axis_index("az")
    rows = naz
    length = SECTOR * naz
    quads = length // 128
    total = nax * rows
    inside = pl.ds(TOP, SECTOR)

    loads = {}
    for index, (name, source, target) in enumerate((
        ("gas", gas_hbm, pad.at[0, pl.ds(1, rows), inside]),
        ("tr", tr_hbm, tr),
        ("heat", heat_hbm, heat),
        ("bed", bed_hbm, bed),
        ("sel", sel_hbm, sel),
        ("th", th_hbm, th),
        ("wall", wall_hbm, wall),
        ("hh", hh_hbm, hh),
        ("hl", hl_hbm, hl),
        ("inv", inv_hbm, inv),
    )):
        loads[name] = pltpu.make_async_copy(source, target, load_sem.at[index])
        loads[name].start()

    barrier = pltpu.get_barrier_semaphore()

    def greet(to_ax, to_az):
        pl.semaphore_signal(barrier, inc=1, device_id=(to_ax, to_az), device_id_type=MESH)

    @pl.loop(1, naz)
    def _(k):
        greet(ax, lax.rem(az + k, naz))

    @pl.loop(1, nax)
    def _(k):
        greet(lax.rem(ax + k, nax), az)

    near_low = az < 3
    at_edge = jnp.logical_or(near_low, az >= naz - 3)
    beside = lax.rem(jnp.where(near_low, ax + nax - 1, ax + 1), nax)

    @pl.when(at_edge)
    def _():
        @pl.loop(0, naz)
        def _(k):
            greet(beside, k)

    lane = lax.broadcasted_iota(jnp.int32, (naz, 128), 1)
    sector = lax.broadcasted_iota(jnp.int32, (naz, 128), 0)
    cell = lane % SECTOR
    group = lane // SECTOR

    def tile_row(row):
        parts = [jnp.broadcast_to(row[:, 128 * q : 128 * q + 128], (4, 128)) for q in range(quads)]
        value = jnp.concatenate(parts, axis=0)
        turn = (sector - group) % 4
        result = value
        for k in range(1, 4):
            result = jnp.where(turn == k, roll_lanes(value, -SECTOR * k), result)
        return result

    def flatten(value):
        result = jnp.zeros_like(value)
        for p in range(4):
            moved = roll_lanes(value, SECTOR * (p - 2))
            result = jnp.where(jnp.logical_and(sector % 4 == p, group == p), moved, result)
        parts = [jnp.sum(result[4 * q : 4 * q + 4], axis=0, keepdims=True) for q in range(quads)]
        return jnp.concatenate(parts, axis=1)

    loads["th"].wait()
    theta0 = th[...]
    theta0_tiled = tile_row(theta0)
    tht[0] = theta0_tiled

    loads["gas"].wait()
    loads["tr"].wait()
    loads["heat"].wait()
    loads["bed"].wait()
    loads["sel"].wait()
    gas = pad[0, 1 : rows + 1, TOP : TOP + SECTOR, :].reshape(rows * SECTOR, 128)
    gas_high, gas_low = split(gas)
    stacked = jnp.concatenate(
        [gas_high, gas_low] + [tr[j].reshape(rows * SECTOR, 128) for j in range(3)], axis=1
    )
    near = lax.dot_general(
        sel[...], stacked, (((1,), (1,)), ((), ())), preferred_element_type=F32
    )
    turned = [near] + [roll_lanes(near, -SECTOR * k) for k in range(1, 4)]
    coded = jnp.where(bed[...] == 1, -heat[...], heat[...])
    coded = jnp.concatenate([coded] * 4, axis=1)
    coded_high = coded.astype(BF16).astype(F32)
    coded_low = coded - coded_high
    field8 = lax.broadcasted_iota(jnp.int32, (8, 128), 0)
    for i in range(rows):
        parts = []
        for part, first in enumerate(WINDOWS):
            start = (i + first) % rows
            quad = start // 4
            parts.append(turned[start % 4][8 * part : 8 * part + 8, 128 * quad : 128 * quad + 128])
        parts[3] = jnp.where(field8 == 3, coded_high[i : i + 1], parts[3])
        parts[3] = jnp.where(field8 == 4, coded_low[i : i + 1], parts[3])
        msg[i] = jnp.concatenate(parts, axis=0).astype(BF16)

    def stage_columns(step):
        col_out[step, 0] = pad[step, 1 : rows + 1, TOP, :]
        col_out[step, 1] = pad[step, 1 : rows + 1, TOP + SECTOR - 1, :]

    stage_columns(0)

    pl.semaphore_wait(barrier, naz - 1 + nax - 1 + 6)

    def remote(source, target, send, receive, to_ax, to_az):
        return pltpu.make_async_remote_copy(
            src_ref=source, dst_ref=target, send_sem=send, recv_sem=receive,
            device_id=(to_ax, to_az), device_id_type=MESH,
        )

    def wait_bytes(ref, sem):
        pltpu.make_async_copy(ref, ref, sem).wait()

    @pl.loop(1, naz)
    def _(k):
        to = lax.rem(az + k, naz)
        remote(msg.at[to], recv.at[az], msg_sem.at[0], msg_sem.at[1], ax, to).start()

    for low in (True, False):
        to_ax = lax.rem(ax + 1, nax) if low else lax.rem(ax + nax - 1, nax)

        @pl.loop(0, 3)
        def _(k):
            to = k if low else naz - 3 + k
            remote(msg.at[to], recv_nb.at[az], nb_sem.at[0], nb_sem.at[1], to_ax, to).start()

    flat = ax * naz + az

    def send_theta(which):
        for slot, offset in enumerate((2, 1, -1, -2)):
            to = lax.rem(flat + offset + total, total)
            remote(
                tht.at[which], thn.at[which, slot], th_sem.at[which, 0], th_sem.at[which, 1],
                lax.div(to, naz), lax.rem(to, naz),
            ).start()

    send_theta(0)

    def halo_copies(step):
        up_ax, down_ax = lax.rem(ax + 1, nax), lax.rem(ax + nax - 1, nax)
        up_az, down_az = lax.rem(az + 1, naz), lax.rem(az + naz - 1, naz)
        return (
            remote(pad.at[step, rows, inside], pad.at[step, 0, inside],
                   halo_ss.at[step, 0], halo_rs.at[step, 0], up_ax, az),
            remote(pad.at[step, 1, inside], pad.at[step, rows + 1, inside],
                   halo_ss.at[step, 1], halo_rs.at[step, 1], down_ax, az),
            remote(col_out.at[step, 1], col_in.at[step, 0],
                   halo_ss.at[step, 2], halo_rs.at[step, 2], ax, up_az),
            remote(col_out.at[step, 0], col_in.at[step, 1],
                   halo_ss.at[step, 3], halo_rs.at[step, 3], ax, down_az),
        )

    def send_halo(step):
        for copy in halo_copies(step):
            copy.start()

    def take_halo(step):
        for copy in halo_copies(step):
            copy.wait()

        @pl.when(ax == 0)
        def _():
            pad[step, 0, inside, :] = jnp.zeros((SECTOR, 128), F32)

        @pl.when(ax == nax - 1)
        def _():
            pad[step, rows + 1, inside, :] = jnp.zeros((SECTOR, 128), F32)

        pad[step, 1 : rows + 1, TOP - 1, :] = col_in[step, 0]
        pad[step, 1 : rows + 1, TOP + SECTOR, :] = col_in[step, 1]

    send_halo(0)
    recv[az] = msg[az]

    def times_table(value):
        high, low = split(value)
        count = value.shape[0]
        both = jnp.dot(jnp.concatenate([high, low], axis=0), hh[...], preferred_element_type=F32)
        return both[:count] + both[count:] + jnp.dot(high, hl[...], preferred_element_type=F32)

    def row_times_table(row):
        high, low = split(row)
        which = lax.broadcasted_iota(jnp.int32, (16, length), 0)
        both = jnp.where(which == 0, high.astype(F32), jnp.where(which == 1, low.astype(F32), 0.0)).astype(BF16)
        first = jnp.dot(both, hh[...], preferred_element_type=F32)
        second = jnp.dot(both, hl[...], preferred_element_type=F32)
        return first[0:1] + first[1:2] + second[0:1]

    loads["wall"].wait()
    loads["hh"].wait()
    loads["hl"].wait()
    layers = wall.shape[0]
    spectral = times_table(wall[...])
    loads["inv"].wait()

    @pl.loop(0, layers // 2)
    def _(pair):
        for j in range(2):
            layer = 2 * pair + j
            blend[pl.ds(layer, 1), :] = jnp.sum(inv[layer] * spectral, axis=0, keepdims=True)

    mode_gain = inv[0, 0:1, :]
    mode_base = blend[0:1, :]

    lane_row = lax.broadcasted_iota(jnp.int32, (SECTOR, 128), 1)

    def sweep(step, outer_edge, store):
        @pl.loop(0, rows)
        def _(x):
            centre = pad[step, x + 1, inside, :]
            west = pad[step, x, inside, :]
            east = pad[step, x + 2, inside, :]
            south = pad[step, x + 1, pl.ds(TOP - 1, SECTOR), :]
            north = pad[step, x + 1, pl.ds(TOP + 1, SECTOR), :]
            inner = jnp.where(lane_row == 0, centre, roll_lanes(centre, 1))
            outer = jnp.where(lane_row == 127, outer_edge(x), roll_lanes(centre, -1))
            store(x, (
                centre
                + tr[0, x].astype(F32) * (west - centre)
                + tr[1, x].astype(F32) * (south - centre)
                + DIFFUSE * (west + east + south + north - 4.0 * centre)
                + RADIAL * (inner + outer - 2.0 * centre)
                + tr[2, x].astype(F32)
            ))

    def store_pad(step):
        def store(x, value):
            pad[step, x + 1, inside, :] = value
        return store

    take_halo(0)
    sweep(0, lambda x: jnp.zeros((SECTOR, 128), F32), store_pad(1))

    wait_bytes(recv.at[pl.ds(0, naz - 1)], msg_sem.at[1])

    @pl.loop(0, naz)
    def _(source):
        fields[pl.ds(pl.multiple_of(source * NFIELD, NFIELD), NFIELD), :] = recv[source].astype(F32)

    @pl.when(at_edge)
    def _():
        wait_bytes(recv_nb, nb_sem.at[1])
        index = lax.broadcasted_iota(jnp.int32, (NFIELD, 128), 0)
        part = index // 8
        first = jnp.where(part == 0, WINDOWS[0], jnp.where(part == 2, WINDOWS[2], 0))
        place = az + first + lax.broadcasted_iota(jnp.int32, (NFIELD, 128), 1) // SECTOR
        own = jnp.logical_and(place >= 0, place < rows)
        own = jnp.logical_or(own, jnp.logical_and(index >= 27, index < 29))

        @pl.loop(0, naz)
        def _(source):
            here = pl.ds(pl.multiple_of(source * NFIELD, NFIELD), NFIELD)
            fields[here, :] = jnp.where(own, fields[here, :], recv_nb[source].astype(F32))

    def field(index):
        return fields[pl.ds(index, naz, stride=NFIELD), :]

    def in_domain(first):
        place = flat + first + group
        return jnp.logical_and(place >= 0, place < total)

    mask_a, mask_b, mask_c = in_domain(-3), in_domain(0), in_domain(-2)
    gas_a = [jnp.where(mask_a, field(j) + field(4 + j), 0.0) for j in range(4)]
    gas_b = [None] + [jnp.where(mask_b, field(8 + j) + field(11 + j), 0.0) for j in range(3)]
    coef_c = [[field(16 + j) for j in range(3)], [field(19 + j) for j in range(3)]]
    coef_d = [field(24 + j) for j in range(3)]
    coef_125 = [roll_lanes(field(14), 64), roll_lanes(field(15), 64), field(22)]
    coupling = field(27) + field(28)

    def stencil(coef, centre, west, east, inner, outer):
        south = jnp.where(cell == 0, pltpu.roll(roll_lanes(centre, -31), 1, 0), roll_lanes(centre, 1))
        north = jnp.where(
            cell == SECTOR - 1, pltpu.roll(roll_lanes(centre, 31), naz - 1, 0), roll_lanes(centre, -1)
        )
        return (
            centre
            + coef[0] * (west - centre)
            + coef[1] * (south - centre)
            + DIFFUSE * (west + east + south + north - 4.0 * centre)
            + RADIAL * (inner + outer - 2.0 * centre)
            + coef[2]
        )

    centres, easts = [], []
    for j in range(4):
        centre = roll_lanes(gas_a[j], -32)
        east = roll_lanes(gas_a[j], -64)
        if j:
            centre = jnp.where(group == 3, roll_lanes(gas_b[j], 64), centre)
            east = jnp.where(group >= 2, roll_lanes(gas_b[j], 32), east)
        centres.append(centre)
        easts.append(east)
    zero = jnp.zeros((naz, 128), F32)
    base_c = jnp.where(mask_c, stencil(coef_c[0], centres[3], gas_a[3], easts[3], centres[2], zero), 0.0)
    base_d = jnp.where(
        mask_b,
        stencil(coef_d, gas_b[3], roll_lanes(gas_b[3], 32), roll_lanes(gas_b[3], -32), gas_b[2], zero), 0.0,
    )
    one_126 = jnp.where(mask_c, stencil(coef_c[1], centres[2], gas_a[2], easts[2], centres[1], centres[3]), 0.0)
    one_125 = stencil(coef_125, centres[1], gas_a[1], easts[1], centres[0], centres[2])

    def flux_row(which, own):
        wait_bytes(thn.at[which], th_sem.at[which, 1])
        edge_c = jnp.where(
            group == 0, thn[which, 0], jnp.where(group == 1, thn[which, 1], jnp.where(group == 2, own, thn[which, 2]))
        )
        edge_d = thn[which, 3]
        one_c = base_c + jnp.where(mask_c, RADIAL * edge_c, 0.0)
        one_d = base_d + jnp.where(mask_b, RADIAL * edge_d, 0.0)
        east = jnp.where(group == 3, roll_lanes(one_d, 32), roll_lanes(one_c, -32))
        two_c = jnp.where(
            mask_c, stencil(coef_c[0], one_c, roll_lanes(one_c, 32), east, one_126, edge_c), 0.0
        )
        two_126 = stencil(coef_c[1], one_126, roll_lanes(one_126, 32), roll_lanes(one_126, -32), one_125, one_c)
        three = stencil(coef_c[0], two_c, roll_lanes(two_c, 32), roll_lanes(two_c, -32), two_126, edge_c)
        return flatten(jnp.where(coupling < 0, -BED_COEF * own, coupling * (three - own)))

    shift = rot_ref[0]
    shift_back = length - shift

    def wall_face(flux):
        modes = row_times_table(pltpu.roll(flux, shift_back, 1))
        face = row_times_table(modes * mode_gain + mode_base)
        return modes, pltpu.roll(face, shift, 1)

    _, face = wall_face(flux_row(0, theta0_tiled))
    residual1 = face - theta0
    theta1 = theta0 + FIRST_RELAX * residual1
    theta1_tiled = tile_row(theta1)
    tht[1] = theta1_tiled
    send_theta(1)

    @pl.loop(1, naz)
    def _(k):
        to = lax.rem(az + k, naz)
        remote(
            tht.at[1, pl.ds(to, 1)], edge.at[pl.ds(az, 1)], edge_sem.at[0], edge_sem.at[1], ax, to
        ).start()

    edge[pl.ds(az, 1), :] = tht[1, pl.ds(az, 1), :]

    modes, face = wall_face(flux_row(1, theta1_tiled))
    residual2 = face - theta1
    change = residual2 - residual1
    top = jnp.sum(residual1 * change, axis=1, keepdims=True)
    bottom = jnp.sum(change * change, axis=1, keepdims=True)
    lane8 = lax.broadcasted_iota(jnp.int32, (8, 128), 1)
    redsrc[0] = jnp.where(lane8 == 0, top, jnp.where(lane8 == 1, bottom, 0.0))

    @pl.loop(1, naz)
    def _(k):
        to = lax.rem(az + k, naz)
        remote(redsrc.at[0], redbuf.at[0, az], red_sem.at[0], red_sem.at[1], ax, to).start()

    redbuf[0, az] = redsrc[0]

    wait_bytes(edge.at[pl.ds(0, naz - 1)], edge_sem.at[1])
    own_cell = lane_row == lax.broadcasted_iota(jnp.int32, (SECTOR, 128), 0)

    @pl.loop(0, rows)
    def _(x):
        value = jnp.sum(jnp.where(own_cell, edge[pl.ds(x, 1), :], 0.0), axis=1, keepdims=True)
        value = jnp.where(lane_row == 127, value, 0.0)
        ebuf[x] = value
        pad[1, x + 1, inside, :] = pad[1, x + 1, inside, :] + RADIAL * value

    stage_columns(1)
    send_halo(1)

    wall_res[...] = times_table(blend[...] + inv[:, 0, :] * modes)
    wall_copy = pltpu.make_async_copy(wall_res, wall_out, out_sem.at[0])
    wall_copy.start()

    wait_bytes(redbuf.at[0, pl.ds(0, naz - 1)], red_sem.at[1])
    redsrc[1] = jnp.sum(redbuf[0, 0:naz], axis=0)

    @pl.loop(1, nax)
    def _(k):
        to = lax.rem(ax + k, nax)
        remote(redsrc.at[1], redbuf.at[1, ax], red_sem.at[2], red_sem.at[3], to, az).start()

    redbuf[1, ax] = redsrc[1]

    take_halo(1)
    sweep(1, lambda x: ebuf[x], store_pad(2))
    stage_columns(2)
    send_halo(2)

    wait_bytes(redbuf.at[1, pl.ds(0, nax - 1)], red_sem.at[3])
    sums = jnp.sum(redbuf[1, 0:nax], axis=0)
    top = jnp.sum(jnp.where(lane8 == 0, sums, 0.0)[0:1], axis=1, keepdims=True)
    bottom = jnp.sum(jnp.where(lane8 == 1, sums, 0.0)[0:1], axis=1, keepdims=True)
    relax = -FIRST_RELAX * top / (bottom + TINY)
    th[...] = theta1 + relax * residual2
    th_copy = pltpu.make_async_copy(th, th_out, out_sem.at[1])
    th_copy.start()

    take_halo(2)

    def store_result(x, value):
        gas_res[x] = value

    sweep(2, lambda x: ebuf[x], store_result)
    gas_copy = pltpu.make_async_copy(gas_res, gas_out, out_sem.at[2])
    gas_copy.start()

    wait_bytes(msg.at[pl.ds(0, naz - 1)], msg_sem.at[0])
    wait_bytes(msg.at[pl.ds(0, 6)], nb_sem.at[0])
    for which in range(2):
        wait_bytes(thn.at[which], th_sem.at[which, 0])
    wait_bytes(edge.at[pl.ds(0, naz - 1)], edge_sem.at[0])
    wait_bytes(redbuf.at[0, pl.ds(0, naz - 1)], red_sem.at[0])
    wait_bytes(redbuf.at[1, pl.ds(0, nax - 1)], red_sem.at[2])
    wall_copy.wait()
    th_copy.wait()
    gas_copy.wait()


def on_device(
    nax, naz, gas_init, transport, heat_coef, bed_mask, wall_init, interface_init, inverse_blocks, rotation
):
    rows = gas_init.shape[0]
    layers, length = wall_init.shape[1:]
    table_high, table_low = hartley_parts(length)
    anywhere = pl.BlockSpec(memory_space=pl.ANY)
    dma = pltpu.SemaphoreType.DMA
    gas_now, wall_now, theta = pl.pallas_call(
        functools.partial(kernel, nax, naz),
        out_shape=(
            jax.ShapeDtypeStruct(gas_init.shape, F32),
            jax.ShapeDtypeStruct((layers, length), F32),
            jax.ShapeDtypeStruct((1, length), F32),
        ),
        in_specs=[anywhere] * 7 + [pl.BlockSpec(memory_space=pltpu.SMEM)] + [anywhere] * 3,
        out_specs=(anywhere,) * 3,
        scratch_shapes=[
            pltpu.VMEM((3, rows + 2, SECTOR + 2 * TOP, 128), F32),
            pltpu.VMEM(transport.shape, BF16),
            pltpu.VMEM(heat_coef.shape, F32),
            pltpu.VMEM(bed_mask.shape, jnp.int32),
            pltpu.VMEM((layers, length), F32),
            pltpu.VMEM((1, length), F32),
            pltpu.VMEM((layers, layers, length), F32),
            pltpu.VMEM((length, length), BF16),
            pltpu.VMEM((length, length), BF16),
            pltpu.VMEM((NFIELD, 5 * 128), BF16),
            pltpu.VMEM((rows, NFIELD, 128), BF16),
            pltpu.VMEM((naz, NFIELD, 128), BF16),
            pltpu.VMEM((naz, NFIELD, 128), BF16),
            pltpu.VMEM((naz * NFIELD, 128), F32),
            pltpu.VMEM((2, naz, 128), F32),
            pltpu.VMEM((2, 4, naz, 128), F32),
            pltpu.VMEM((rows, 128), F32),
            pltpu.VMEM((rows, SECTOR, 128), F32),
            pltpu.VMEM((3, 2, rows, 128), F32),
            pltpu.VMEM((3, 2, rows, 128), F32),
            pltpu.VMEM((layers, length), F32),
            pltpu.VMEM((layers, length), F32),
            pltpu.VMEM((rows, SECTOR, 128), F32),
            pltpu.VMEM((2, 8, 128), F32),
            pltpu.VMEM((2, max(nax, naz), 8, 128), F32),
            dma((10,)),
            dma((3,)),
            dma((1,)),
            dma((2,)),
            dma((2,)),
            dma((2, 2)),
            dma((2,)),
            dma((3, 4)),
            dma((3, 4)),
            dma((4,)),
        ],
        compiler_params=pltpu.CompilerParams(
            collective_id=0, has_side_effects=True, vmem_limit_bytes=32 * 1024 * 1024
        ),
        name="kiln_step",
    )(
        gas_init, transport, heat_coef, bed_mask, wall_init.reshape(layers, length), interface_init,
        jnp.transpose(inverse_blocks, (1, 2, 0)), rotation,
        jnp.asarray(table_high), jnp.asarray(table_low), jnp.asarray(selector()),
    )
    return gas_now, wall_now.reshape(1, layers, length), theta


def solution(mesh):
    return jax.shard_map(
        functools.partial(on_device, mesh.shape["ax"], mesh.shape["az"]),
        mesh=mesh,
        in_specs=(
            P("ax", "az", None),
            P(None, "ax", "az", None),
            P("ax", "az"),
            P("ax", "az"),
            P(("ax", "az"), None, None),
            P(("ax", "az"), None),
            P(),
            P(),
        ),
        out_specs=(P("ax", "az", None), P(("ax", "az"), None, None), P(("ax", "az"), None)),
        check_vma=False,
    )
```

profile of v0, /device:TPU:1, one launch (start us, length us, event | category | flops | bytes accessed | tf_op | source)
XLA Modules:
  0.0 50.7 jit_solution(13223035745615810301)
XLA Ops:
  1.3 0.0 copy-start
  1.3 2.3 %copy-done = f32[512,48,48]{0,2,1:T(8,128)S(1)} copy-done((f32[512,48,48]{0,2,1:T(8,128)S(1)}, f32[512,48,48]{0,2,1:T(8,128)}, u32[]{:S(2)}) %copy-start) | copy-done | bytes 4718616
  3.6 0.0 copy-start.1
  3.6 1.0 %copy-done.1 = bf16[512,512]{1,0:T(8,128)(2,1)S(1)} copy-done((bf16[512,512]{1,0:T(8,128)(2,1)S(1)}, bf16[512,512]{1,0:T(8,128)(2,1)}, u32[]{:S(2)}) %copy-start.1) | copy-done | bytes 524312
  4.7 0.0 copy-start.2
  4.7 1.0 %copy-done.2 = bf16[512,512]{1,0:T(8,128)(2,1)S(1)} copy-done((bf16[512,512]{1,0:T(8,128)(2,1)S(1)}, bf16[512,512]{1,0:T(8,128)(2,1)}, u32[]{:S(2)}) %copy-start.2) | copy-done | bytes 524312
  5.7 0.0 copy-start.3
  5.7 1.0 %copy-done.3 = bf16[3,16,32,128]{3,2,1,0:T(8,128)(2,1)S(1)} copy-done((bf16[3,16,32,128]{3,2,1,0:T(8,128)(2,1)S(1)}, bf16[3,16,32,128]{3,2,1,0:T(8,128)(2,1)}, u32[]{:S(2)}) %copy-start.3) | copy-done | bytes 393240
  6.7 0.0 copy-start.4
  6.7 0.9 %copy-done.4 = f32[16,32,128]{2,1,0:T(8,128)S(1)} copy-done((f32[16,32,128]{2,1,0:T(8,128)S(1)}, f32[16,32,128]{2,1,0:T(8,128)}, u32[]{:S(2)}) %copy-start.4) | copy-done | bytes 262168
  7.6 0.0 copy-start.5
  7.7 0.9 %copy-done.5 = f32[1,48,512]{2,1,0:T(8,128)S(1)} copy-done((f32[1,48,512]{2,1,0:T(8,128)S(1)}, f32[1,48,512]{2,1,0:T(8,128)}, u32[]{:S(2)}) %copy-start.5) | copy-done | bytes 98328
  8.5 0.0 copy-start.6
  8.5 0.8 %copy-done.6 = bf16[32,640]{1,0:T(8,128)(2,1)S(1)} copy-done((bf16[32,640]{1,0:T(8,128)(2,1)S(1)}, bf16[32,640]{1,0:T(8,128)(2,1)}, u32[]{:S(2)}) %copy-start.6) | copy-done | bytes 40984
  9.3 0.0 copy-start.7
  9.3 0.7 %copy-done.7 = f32[16,32]{1,0:T(8,128)S(1)} copy-done((f32[16,32]{1,0:T(8,128)S(1)}, f32[16,32]{1,0:T(8,128)}, u32[]{:S(2)}) %copy-start.7) | copy-done | bytes 2072
  10.0 0.0 copy-start.8
  10.0 0.7 %copy-done.8 = s32[16,32]{1,0:T(8,128)S(1)} copy-done((s32[16,32]{1,0:T(8,128)S(1)}, s32[16,32]{1,0:T(8,128)}, u32[]{:S(2)}) %copy-start.8) | copy-done | bytes 2072
  10.7 0.0 copy-start.9
  10.7 0.7 %copy-done.9 = f32[1,512]{1,0:T(1,128)S(1)} copy-done((f32[1,512]{1,0:T(1,128)S(1)}, f32[1,512]{1,0:T(1,128)}, u32[]{:S(2)}) %copy-start.9) | copy-done | bytes 2072
  11.4 37.4 %kiln_step.1 = (f32[16,32,128]{2,1,0:T(8,128)S(1)}, f32[48,512]{1,0:T(8,128)S(1)}, f32[1,512]{1,0:T(1,128)S(1)}) custom-call(f32[16,32,128]{2,1,0:T(8,128)S(1)} %copy-done.4, bf16[3,16,32,128]{3,2,1,0:T(8,128)(2,1)S(1)} %copy-done.3, f32[16,32]{1,0:T(8,128)S(1)} %copy-done.7, s32[16,32]{1,0:T(8,128)S(1)} %copy-done.8, f32[48,512]{1,0:T(8,128)S(1)} %bitcast.5, ...), custom_call_target="tpu_custom_call" | custom-call | tf_op jit(solution)/shard_map/kiln_step/pallas_call | solution.py:501
  48.8 0.7 %copy.18 = f32[16,32,128]{2,1,0:T(8,128)} copy(f32[16,32,128]{2,1,0:T(8,128)S(1)} %get-tuple-element.12) | data formatting | bytes 524288
  49.5 0.6 %copy.19 = f32[1,48,512]{2,1,0:T(8,128)} copy(f32[1,48,512]{2,1,0:T(8,128)S(1)} %bitcast.4) | data formatting | bytes 196608
  50.1 0.6 %copy.20 = f32[1,512]{1,0:T(1,128)} copy(f32[1,512]{1,0:T(1,128)S(1)} %get-tuple-element.14) | data formatting | bytes 4096
Async XLA Ops:
  1.3 2.3 %copy-start = (f32[512,48,48]{0,2,1:T(8,128)S(1)}, f32[512,48,48]{0,2,1:T(8,128)}, u32[]{:S(2)}) copy-start(f32[512,48,48]{0,2,1:T(8,128)} %param.17) | copy-start | bytes 14155780
  3.6 1.0 %copy-start.1 = (bf16[512,512]{1,0:T(8,128)(2,1)S(1)}, bf16[512,512]{1,0:T(8,128)(2,1)}, u32[]{:S(2)}) copy-start(bf16[512,512]{1,0:T(8,128)(2,1)} %constant.7.clone.hl_hbm) | copy-start | bytes 1572868
  4.7 1.0 %copy-start.2 = (bf16[512,512]{1,0:T(8,128)(2,1)S(1)}, bf16[512,512]{1,0:T(8,128)(2,1)}, u32[]{:S(2)}) copy-start(bf16[512,512]{1,0:T(8,128)(2,1)} %constant.6.clone.hh_hbm) | copy-start | bytes 1572868
  5.7 1.0 %copy-start.3 = (bf16[3,16,32,128]{3,2,1,0:T(8,128)(2,1)S(1)}, bf16[3,16,32,128]{3,2,1,0:T(8,128)(2,1)}, u32[]{:S(2)}) copy-start(bf16[3,16,32,128]{3,2,1,0:T(8,128)(2,1)} %tr_hbm.1) | copy-start | bytes 1179652
  6.7 0.9 %copy-start.4 = (f32[16,32,128]{2,1,0:T(8,128)S(1)}, f32[16,32,128]{2,1,0:T(8,128)}, u32[]{:S(2)}) copy-start(f32[16,32,128]{2,1,0:T(8,128)} %gas_hbm.1) | copy-start | bytes 786436
  7.6 0.9 %copy-start.5 = (f32[1,48,512]{2,1,0:T(8,128)S(1)}, f32[1,48,512]{2,1,0:T(8,128)}, u32[]{:S(2)}) copy-start(f32[1,48,512]{2,1,0:T(8,128)} %param.15) | copy-start | bytes 294916
  8.5 0.8 %copy-start.6 = (bf16[32,640]{1,0:T(8,128)(2,1)S(1)}, bf16[32,640]{1,0:T(8,128)(2,1)}, u32[]{:S(2)}) copy-start(bf16[32,640]{1,0:T(8,128)(2,1)} %constant.8.clone.sel_hbm) | copy-start | bytes 122884
  9.3 0.7 %copy-start.7 = (f32[16,32]{1,0:T(8,128)S(1)}, f32[16,32]{1,0:T(8,128)}, u32[]{:S(2)}) copy-start(f32[16,32]{1,0:T(8,128)} %heat_hbm.1) | copy-start | bytes 6148
  10.0 0.7 %copy-start.8 = (s32[16,32]{1,0:T(8,128)S(1)}, s32[16,32]{1,0:T(8,128)}, u32[]{:S(2)}) copy-start(s32[16,32]{1,0:T(8,128)} %bed_hbm.1) | copy-start | bytes 6148
  10.7 0.7 %copy-start.9 = (f32[1,512]{1,0:T(1,128)S(1)}, f32[1,512]{1,0:T(1,128)}, u32[]{:S(2)}) copy-start(f32[1,512]{1,0:T(1,128)} %th_hbm.1) | copy-start | bytes 6148
where the time goes:
time: 51.2 us; the launch traced here: 50.7 us
  Pallas kernels  37.4 us (73%)
  local copies, waits for them, and re-layouts  12 us (23%)
  between operations  1.31 us (3%)
    pallas_call x1, Pallas kernels, on_device(): pl.pallas_call(functools.partial(kernel, nax, naz), out_shape=(jax.ShapeD...  37.4 us
    unnamed x23, local copies, waits for them, and re-layouts  12 us

commit v1 on v0

v1 whole, which is shorter than its diff:
```python
import functools

import jax
import jax.numpy as jnp
import ml_dtypes
import numpy as np
from jax import lax
from jax.experimental import pallas as pl
from jax.experimental.pallas import tpu as pltpu
from jax.sharding import PartitionSpec as P

DIFFUSE = 0.04
RADIAL = 0.06
BED_COEF = 0.8
FIRST_RELAX = 0.5
TINY = 1e-06
MESH = pl.DeviceIdType.MESH
F32 = jnp.float32
BF16 = jnp.bfloat16
SECTOR = 32
TOP = 8
COUPLING, LOW = "coupling", "low"
GAS = [(part, r) for part in (0, 1) for r in (124, 125, 126, 127)]
WALLSIDE = [(2, 127), (3, 127), (4, 127), (2, 126), (3, 126), (4, 126), COUPLING, LOW]
FIELDS = (
    GAS
    + WALLSIDE
    + GAS
    + [(2, 125), (3, 125), (4, 125)] * 2 + [(4, 127), None]
    + [(part, r) for part in (0, 1) for r in (125, 126, 127)] + [(2, 127), (3, 127)]
    + WALLSIDE
)
NFIELD = len(FIELDS)
FIRSTS = [-5] * 8 + [-4] * 8 + [-1] * 8 + [-4] * 3 + [0] * 3 + [2] * 2 + [2] * 8 + [0] * 8
REACH = 5


def hartley_parts(length):
    positions = np.arange(length, dtype=np.int64)
    phases = 2.0 * np.pi / length * ((positions[:, None] * positions[None, :]) % length)
    table = ((np.cos(phases) + np.sin(phases)) / np.sqrt(length)).astype(np.float32)
    high = table.astype(ml_dtypes.bfloat16)
    low = (table - high.astype(np.float32)).astype(ml_dtypes.bfloat16)
    return high, low


def selector():
    table = np.zeros((NFIELD, 5 * 128), np.float32)
    for row, field in enumerate(FIELDS):
        if isinstance(field, tuple):
            table[row, field[0] * 128 + field[1]] = 1.0
    return table.astype(ml_dtypes.bfloat16)


def split(value):
    high = value.astype(BF16)
    return high, (value - high.astype(F32)).astype(BF16)


def roll_lanes(value, amount):
    amount = amount % value.shape[1]
    return pltpu.roll(value, amount, 1) if amount else value


def kernel(
    nax, naz,
    gas_hbm, tr_hbm, heat_hbm, bed_hbm, wall_hbm, th_hbm, inv_hbm, rot_ref, hh_hbm, hl_hbm, sel_hbm,
    gas_res, wall_res, th_res,
    pad, tr, heat, bed, wall, th, inv, hh, hl, sel,
    msg, recv, recv_nb, fields, th_rows, base_rows, window, edge, coef_out, coef_in, col_out, col_in, blend,
    redsrc, redbuf,
    load_sem, msg_sem, nb_sem, th_sem, base_sem, edge_sem, halo_ss, halo_rs, coef_ss, coef_rs, red_sem,
):
    ax, az = lax.axis_index("ax"), lax.axis_index("az")
    rows = naz
    length = SECTOR * naz
    quads = length // 128
    total = nax * rows
    flat = ax * naz + az
    up_ax, down_ax = lax.rem(ax + 1, nax), lax.rem(ax + nax - 1, nax)
    up_az, down_az = lax.rem(az + 1, naz), lax.rem(az + naz - 1, naz)
    inside = pl.ds(TOP, SECTOR)

    loads = {}
    for index, (name, source, target) in enumerate((
        ("gas", gas_hbm, pad.at[0, pl.ds(1, rows), inside]),
        ("tr", tr_hbm, tr),
        ("heat", heat_hbm, heat),
        ("bed", bed_hbm, bed),
        ("sel", sel_hbm, sel),
        ("th", th_hbm, th),
        ("wall", wall_hbm, wall),
        ("hh", hh_hbm, hh),
        ("hl", hl_hbm, hl),
        ("inv", inv_hbm, inv),
    )):
        loads[name] = pltpu.make_async_copy(source, target, load_sem.at[index])
        loads[name].start()

    barrier = pltpu.get_barrier_semaphore()

    def greet(to_ax, to_az):
        pl.semaphore_signal(barrier, inc=1, device_id=(to_ax, to_az), device_id_type=MESH)

    @pl.loop(1, naz)
    def _(k):
        greet(ax, lax.rem(az + k, naz))

    @pl.loop(1, nax)
    def _(k):
        greet(lax.rem(ax + k, nax), az)

    low_edge, high_edge = az < REACH, az >= naz - REACH
    at_edge = jnp.logical_or(low_edge, high_edge)
    beside = jnp.where(low_edge, down_ax, up_ax)
    at_rim = jnp.logical_or(az < 2, az >= naz - 2)

    @pl.when(at_edge)
    def _():
        @pl.loop(0, naz)
        def _(k):
            greet(beside, k)

    for k in range(2):
        greet(up_ax, k)
        greet(down_ax, naz - 2 + k)

    lane = lax.broadcasted_iota(jnp.int32, (naz, 128), 1)
    sector = lax.broadcasted_iota(jnp.int32, (naz, 128), 0)
    cell = lane % SECTOR
    group = lane // SECTOR
    turn = sector % 4

    def tile_rows(values):
        result = jnp.zeros((naz, 128), F32)
        for g, row in enumerate(values):
            if row is None:
                continue
            wide = jnp.concatenate(
                [jnp.broadcast_to(row[:, 128 * q : 128 * q + 128], (4, 128)) for q in range(quads)], axis=0
            )
            for p in range(4):
                here = jnp.logical_and(turn == p, group == g)
                result = jnp.where(here, roll_lanes(wide, SECTOR * (g - p)), result)
        return result

    def flatten(value, groups):
        moved = [roll_lanes(value, SECTOR * k) for k in range(4)]
        found = []
        for g in groups:
            result = jnp.zeros_like(value)
            for p in range(4):
                result = jnp.where(jnp.logical_and(turn == p, group == p), moved[(p - g) % 4], result)
            parts = [jnp.sum(result[4 * q : 4 * q + 4], axis=0, keepdims=True) for q in range(quads)]
            found.append(jnp.concatenate(parts, axis=1))
        return found

    def four_times(value):
        return jnp.concatenate([value] * 4, axis=1)

    loads["th"].wait()
    theta0 = th[...]
    th_rows[4:5, :] = theta0

    for name in ("gas", "tr", "heat", "bed", "sel"):
        loads[name].wait()
    gas = pad[0, 1 : rows + 1, TOP : TOP + SECTOR, :].reshape(rows * SECTOR, 128)
    gas_high, gas_low = split(gas)
    stacked = jnp.concatenate(
        [gas_high, gas_low] + [tr[j].reshape(rows * SECTOR, 128) for j in range(3)], axis=1
    )
    near = lax.dot_general(
        sel[...], stacked, (((1,), (1,)), ((), ())), preferred_element_type=F32
    )
    coded = four_times(jnp.where(bed[...] == 1, -heat[...], heat[...]))
    coded, = flatten(coded, (0,))
    coded_high = coded.astype(BF16).astype(F32)
    field_row = lax.broadcasted_iota(jnp.int32, (NFIELD, rows * SECTOR), 0)
    for index, one in enumerate(FIELDS):
        if one == COUPLING:
            near = jnp.where(field_row == index, coded_high, near)
        if one == LOW:
            near = jnp.where(field_row == index, coded - coded_high, near)
    turned = [near] + [roll_lanes(near, -SECTOR * k) for k in range(1, 4)]
    field8 = lax.broadcasted_iota(jnp.int32, (8, 128), 0)
    for i in range(rows):
        parts = []
        for part in range(NFIELD // 8):
            value = None
            for j in range(8):
                first = FIRSTS[8 * part + j]
                if j and first == FIRSTS[8 * part + j - 1]:
                    continue
                start = (i + first) % rows
                piece = turned[start % 4][8 * part : 8 * part + 8, 128 * (start // 4) : 128 * (start // 4) + 128]
                value = piece if value is None else jnp.where(field8 >= j, piece, value)
            parts.append(value)
        msg[i] = jnp.concatenate(parts, axis=0).astype(BF16)

    def stage_columns(step):
        col_out[step, 0] = pad[step, 1 : rows + 1, TOP, :]
        col_out[step, 1] = pad[step, 1 : rows + 1, TOP + SECTOR - 1, :]

    stage_columns(0)
    courant = [tile_rows([near[index : index + 1]] * 4) for index in (8, 9, 11, 12)]
    coef_out[0] = courant[0]
    coef_out[1] = courant[1]

    pl.semaphore_wait(barrier, naz - 1 + nax - 1 + 2 * REACH + jnp.where(at_rim, naz, 0))

    def remote(source, target, send, receive, to_ax, to_az):
        return pltpu.make_async_remote_copy(
            src_ref=source, dst_ref=target, send_sem=send, recv_sem=receive,
            device_id=(to_ax, to_az), device_id_type=MESH,
        )

    def wait_bytes(ref, sem):
        pltpu.make_async_copy(ref, ref, sem).wait()

    @pl.loop(0, REACH)
    def _(k):
        remote(msg.at[k, pl.ds(0, 32)], recv_nb.at[az], nb_sem.at[0], nb_sem.at[1], up_ax, k).start()
        high = naz - REACH + k
        remote(msg.at[high, pl.ds(16, 32)], recv_nb.at[az], nb_sem.at[0], nb_sem.at[1], down_ax, high).start()

    @pl.loop(1, naz)
    def _(k):
        to = lax.rem(az + k, naz)
        remote(msg.at[to], recv.at[az], msg_sem.at[0], msg_sem.at[1], ax, to).start()

    def send_row(ref, slot, reach, sems):
        for offset in range(-reach, reach + 1):
            if offset:
                to = lax.rem(flat + offset + total, total)
                remote(
                    ref.at[pl.ds(slot, 1)], ref.at[pl.ds(slot - offset, 1)], sems.at[0], sems.at[1],
                    lax.div(to, naz), lax.rem(to, naz),
                ).start()

    send_row(th_rows, 4, 4, th_sem)

    def times_table(value):
        high, low = split(value)
        count = value.shape[0]
        both = jnp.dot(jnp.concatenate([high, low], axis=0), hh[...], preferred_element_type=F32)
        return both[:count] + both[count:] + jnp.dot(high, hl[...], preferred_element_type=F32)

    def rows_times_table(value):
        count = value.shape[0]
        value = jnp.concatenate([value, jnp.zeros((8 - count, length), F32)], axis=0)
        high = value.astype(BF16).astype(F32)
        both = jnp.concatenate([high, value - high], axis=0).astype(BF16)
        first = jnp.dot(both, hh[...], preferred_element_type=F32)
        second = jnp.dot(both, hl[...], preferred_element_type=F32)
        return (first[0:8] + first[8:16] + second[0:8])[:count]

    loads["wall"].wait()
    loads["hh"].wait()
    loads["hl"].wait()
    layers = wall.shape[0]
    spectral = times_table(wall[...])
    loads["inv"].wait()
    mode_gain = inv[0, 0:1, :]
    mode_base = jnp.sum(inv[0] * spectral, axis=0, keepdims=True)
    base_rows[2:3, :] = mode_base
    send_row(base_rows, 2, 2, base_sem)

    def halo_copies(step):
        return (
            remote(pad.at[step, rows, inside], pad.at[step, 0, inside],
                   halo_ss.at[step, 0], halo_rs.at[step, 0], up_ax, az),
            remote(pad.at[step, 1, inside], pad.at[step, rows + 1, inside],
                   halo_ss.at[step, 1], halo_rs.at[step, 1], down_ax, az),
            remote(col_out.at[step, 1], col_in.at[step, 0],
                   halo_ss.at[step, 2], halo_rs.at[step, 2], ax, up_az),
            remote(col_out.at[step, 0], col_in.at[step, 1],
                   halo_ss.at[step, 3], halo_rs.at[step, 3], ax, down_az),
        )

    def send_halo(step):
        for copy in halo_copies(step):
            copy.start()

    def take_halo(step):
        for copy in halo_copies(step):
            copy.wait()

        @pl.when(ax == 0)
        def _():
            pad[step, 0, inside, :] = jnp.zeros((SECTOR, 128), F32)

        @pl.when(ax == nax - 1)
        def _():
            pad[step, rows + 1, inside, :] = jnp.zeros((SECTOR, 128), F32)

        pad[step, 1 : rows + 1, TOP - 1, :] = col_in[step, 0]
        pad[step, 1 : rows + 1, TOP + SECTOR, :] = col_in[step, 1]

    send_halo(0)
    coef_copies = [
        remote(coef_out, coef_in.at[slot], coef_ss.at[slot], coef_rs.at[slot], to_ax, to_az)
        for slot, (to_ax, to_az) in enumerate(((up_ax, az), (down_ax, az), (ax, up_az), (ax, down_az)))
    ]
    for copy in coef_copies:
        copy.start()
    recv[az] = msg[az]

    @pl.loop(0, layers // 2)
    def _(pair):
        for j in range(2):
            layer = 2 * pair + j
            blend[pl.ds(layer, 1), :] = jnp.sum(inv[layer] * spectral, axis=0, keepdims=True)

    lane_row = lax.broadcasted_iota(jnp.int32, (SECTOR, 128), 1)

    def sweep(step, store):
        @pl.loop(0, rows)
        def _(x):
            centre = pad[step, x + 1, inside, :]
            west = pad[step, x, inside, :]
            east = pad[step, x + 2, inside, :]
            south = pad[step, x + 1, pl.ds(TOP - 1, SECTOR), :]
            north = pad[step, x + 1, pl.ds(TOP + 1, SECTOR), :]
            inner = jnp.where(lane_row == 0, centre, roll_lanes(centre, 1))
            outer = jnp.where(lane_row == 127, 0.0, roll_lanes(centre, -1))
            store(x, (
                centre
                + tr[0, x].astype(F32) * (west - centre)
                + tr[1, x].astype(F32) * (south - centre)
                + DIFFUSE * (west + east + south + north - 4.0 * centre)
                + RADIAL * (inner + outer - 2.0 * centre)
                + tr[2, x].astype(F32)
            ))

    def store_pad(step):
        def store(x, value):
            pad[step, x + 1, inside, :] = value
        return store

    take_halo(0)
    sweep(0, store_pad(1))
    stage_columns(1)
    send_halo(1)

    wait_bytes(recv.at[pl.ds(0, naz - 1)], msg_sem.at[1])

    @pl.loop(0, naz)
    def _(source):
        fields[pl.ds(pl.multiple_of(source * NFIELD, NFIELD), NFIELD), :] = recv[source].astype(F32)

    def merge(start):
        firsts = jnp.zeros((32, 128), jnp.int32)
        index = lax.broadcasted_iota(jnp.int32, (32, 128), 0)
        for j in range(32):
            if j == 0 or FIRSTS[start + j] != FIRSTS[start + j - 1]:
                firsts = jnp.where(index >= j, FIRSTS[start + j], firsts)
        place = az + firsts + lax.broadcasted_iota(jnp.int32, (32, 128), 1) // SECTOR
        own = jnp.logical_and(place >= 0, place < rows)

        @pl.loop(0, naz)
        def _(source):
            here = pl.ds(pl.multiple_of(source * NFIELD + start, 16), 32)
            fields[here, :] = jnp.where(own, fields[here, :], recv_nb[source].astype(F32))

    @pl.when(low_edge)
    def _():
        wait_bytes(recv_nb, nb_sem.at[1])
        merge(0)

    @pl.when(high_edge)
    def _():
        wait_bytes(recv_nb, nb_sem.at[1])
        merge(16)

    def field(index):
        return fields[pl.ds(index, naz, stride=NFIELD), :]

    def in_domain(first):
        place = flat + first + group
        return jnp.logical_and(place >= 0, place < total)

    def masked(first, value):
        return jnp.where(in_domain(first), value, 0.0)

    gas_p = [masked(-5, field(j) + field(4 + j)) for j in range(4)]
    gas_q = [masked(-1, field(16 + j) + field(20 + j)) for j in range(4)]
    gas_r = [None] + [masked(2, field(32 + j) + field(35 + j)) for j in range(3)]
    coef_127 = [[field(8 + j) for j in range(3)], [field(40 + j) for j in range(3)]]
    coef_127.append([roll_lanes(field(j), -64) for j in (38, 39, 30)])
    coef_126 = [[field(11 + j) for j in range(3)], [field(43 + j) for j in range(3)]]
    coef_125 = [[field(24 + j) for j in range(3)], [field(27 + j) for j in range(3)]]
    coupling = [field(14) + field(15), field(46) + field(47)]

    def stencil(coef, centre, west, east, inner, outer):
        south = jnp.where(cell == 0, pltpu.roll(roll_lanes(centre, -31), 1, 0), roll_lanes(centre, 1))
        north = jnp.where(
            cell == SECTOR - 1, pltpu.roll(roll_lanes(centre, 31), naz - 1, 0), roll_lanes(centre, -1)
        )
        return (
            centre
            + coef[0] * (west - centre)
            + coef[1] * (south - centre)
            + DIFFUSE * (west + east + south + north - 4.0 * centre)
            + RADIAL * (inner + outer - 2.0 * centre)
            + coef[2]
        )

    def windows(p, q, r):
        if r is None:
            r = jnp.zeros_like(q)
        centres = (
            jnp.where(group == 3, roll_lanes(q, 96), roll_lanes(p, -32)),
            jnp.where(group == 3, roll_lanes(r, 64), roll_lanes(q, -32)),
        )
        easts = (
            jnp.where(group >= 2, roll_lanes(q, 64), roll_lanes(p, -64)),
            jnp.where(group >= 2, roll_lanes(r, 32), roll_lanes(q, -64)),
        )
        return centres, (p, q), easts

    def shifted(zero, one, two=None):
        west = (roll_lanes(zero, 32), jnp.where(group == 0, roll_lanes(zero, 32), roll_lanes(one, 32)))
        last = roll_lanes(one, -32)
        if two is not None:
            last = jnp.where(group == 3, roll_lanes(two, 96), last)
        east = (jnp.where(group == 3, roll_lanes(one, -32), roll_lanes(zero, -32)), last)
        return west, east

    none = jnp.zeros((naz, 128), F32)
    centre_124 = windows(gas_p[0], gas_q[0], None)[0]
    centre_125, west_125, east_125 = windows(gas_p[1], gas_q[1], gas_r[1])
    centre_126, west_126, east_126 = windows(gas_p[2], gas_q[2], gas_r[2])
    centre_127, west_127, east_127 = windows(gas_p[3], gas_q[3], gas_r[3])
    firsts = (-4, 0, 4)
    base = [
        masked(firsts[w], stencil(coef_127[w], centre_127[w], west_127[w], east_127[w], centre_126[w], none))
        for w in range(2)
    ]
    base.append(masked(4, stencil(
        coef_127[2], roll_lanes(gas_r[3], -64), roll_lanes(gas_r[3], -32), roll_lanes(gas_r[3], -96),
        roll_lanes(gas_r[2], -64), none,
    )))
    one_126 = [
        masked(firsts[w], stencil(coef_126[w], centre_126[w], west_126[w], east_126[w], centre_125[w], centre_127[w]))
        for w in range(2)
    ]
    one_125 = [
        stencil(coef_125[w], centre_125[w], west_125[w], east_125[w], centre_124[w], centre_126[w]) for w in range(2)
    ]
    west_one_126, east_one_126 = shifted(*one_126)

    def near_flux(edges, wanted):
        one = [base[w] + masked(firsts[w], RADIAL * edges[w]) for w in range(3)]
        west, east = shifted(*one)
        two = [
            masked(firsts[w], stencil(coef_127[w], one[w], west[w], east[w], one_126[w], edges[w])) for w in range(2)
        ]
        west, east = shifted(*two)
        result = []
        for w in wanted:
            two_126 = stencil(coef_126[w], one_126[w], west_one_126[w], east_one_126[w], one_125[w], one[w])
            three = stencil(coef_127[w], two[w], west[w], east[w], two_126, edges[w])
            result.append(jnp.where(
                coupling[w] < 0, -BED_COEF * edges[w], coupling[w] * (three - edges[w])
            ))
        return result

    shift = rot_ref[0]
    shift_back = length - shift

    def wall_face(flux, without):
        modes = rows_times_table(pltpu.roll(flux, shift_back, 1))
        face = rows_times_table(modes * mode_gain + without)
        return modes, pltpu.roll(face, shift, 1)

    wait_bytes(th_rows.at[pl.ds(0, 8)], th_sem.at[1])
    start = th_rows[0:9, :]
    rows_of = lambda values, *picks: tile_rows([None if k is None else values[k : k + 1] for k in picks])
    flux = near_flux(
        [rows_of(start, 0, 1, 2, 3), rows_of(start, 4, 5, 6, 7), rows_of(start, 8, None, None, None)], (0, 1)
    )
    flux = jnp.concatenate(flatten(flux[0], (2, 3)) + flatten(flux[1], (0, 1, 2)), axis=0)
    wait_bytes(base_rows.at[pl.ds(0, 4)], base_sem.at[1])
    _, face = wall_face(flux, base_rows[0:5, :])
    residual1 = face - start[2:7]
    theta1 = start[2:7] + FIRST_RELAX * residual1
    flux = near_flux(
        [rows_of(theta1, None, None, 0, 1), rows_of(theta1, 2, 3, 4, None), none], (1,)
    )
    modes, face = wall_face(flatten(flux[0], (0,))[0], mode_base)
    residual1 = residual1[2:3]
    theta1 = theta1[2:3]
    residual2 = face - theta1
    change = residual2 - residual1
    top = jnp.sum(residual1 * change, axis=1, keepdims=True)
    bottom = jnp.sum(change * change, axis=1, keepdims=True)
    lane1 = lax.broadcasted_iota(jnp.int32, (1, 128), 1)
    redsrc[0:1] = jnp.where(lane1 == 0, top, jnp.where(lane1 == 1, bottom, 0.0))

    @pl.loop(1, naz)
    def _(k):
        to = lax.rem(az + k, naz)
        remote(redsrc.at[pl.ds(0, 1)], redbuf.at[0, pl.ds(az, 1)], red_sem.at[0], red_sem.at[1], ax, to).start()

    redbuf[0, pl.ds(az, 1), :] = redsrc[0:1]

    turned = [roll_lanes(theta1, -SECTOR * (p - 1)) for p in range(4)]
    window[...] = jnp.concatenate(
        [turned[k % 4][:, 128 * (k // 4) : 128 * (k // 4) + 128] for k in range(naz)], axis=0
    )

    @pl.loop(1, naz)
    def _(k):
        to = lax.rem(az + k, naz)
        remote(
            window.at[pl.ds(to, 1)], edge.at[pl.ds(TOP + az, 1)], edge_sem.at[0], edge_sem.at[1], ax, to
        ).start()

    rim_ax = jnp.where(az < 2, down_ax, up_ax)
    rim_row = jnp.where(az < 2, TOP + rows + az, TOP - naz + az)

    @pl.when(at_rim)
    def _():
        @pl.loop(0, naz)
        def _(k):
            remote(
                window.at[pl.ds(k, 1)], edge.at[pl.ds(rim_row, 1)], edge_sem.at[2], edge_sem.at[3], rim_ax, k
            ).start()

    edge[pl.ds(TOP + az, 1), :] = window[pl.ds(az, 1), :]

    wall_res[...] = times_table(blend[...] + inv[:, 0, :] * modes)

    take_halo(1)
    sweep(1, store_pad(2))
    stage_columns(2)
    send_halo(2)

    wait_bytes(redbuf.at[0, pl.ds(0, naz - 1)], red_sem.at[1])
    redsrc[1:2] = jnp.sum(redbuf[0, 0:naz], axis=0, keepdims=True)

    @pl.loop(1, nax)
    def _(k):
        to = lax.rem(ax + k, nax)
        remote(redsrc.at[pl.ds(1, 1)], redbuf.at[1, pl.ds(ax, 1)], red_sem.at[2], red_sem.at[3], to, az).start()

    redbuf[1, pl.ds(ax, 1), :] = redsrc[1:2]

    take_halo(2)

    def store_result(x, value):
        gas_res[x] = value

    sweep(2, store_result)

    for copy in coef_copies:
        copy.wait()
    wait_bytes(edge.at[pl.ds(0, naz - 1)], edge_sem.at[1])
    wait_bytes(edge.at[pl.ds(0, 4)], edge_sem.at[3])
    tall = rows + 2 * TOP
    place = lax.broadcasted_iota(jnp.int32, (tall, 128), 0)
    row_x = ax * rows + place - TOP
    valid = jnp.logical_and(jnp.logical_and(row_x >= 0, row_x < total),
                            jnp.logical_and(place >= TOP - 2, place < TOP + rows + 2))
    theta = jnp.where(valid, edge[...], 0.0)

    def tall_coef(j):
        middle = jnp.where(group == 0, coef_in[2, j], jnp.where(group == 2, coef_in[3, j], courant[j]))
        below = jnp.broadcast_to(coef_in[0, j, rows - 1 : rows, :], (TOP, 128))
        above = jnp.broadcast_to(coef_in[1, j, 0:1, :], (TOP, 128))
        return jnp.concatenate([below, middle, above], axis=0)

    def tall_only(value):
        return jnp.concatenate([jnp.zeros((TOP, 128), F32), value, jnp.zeros((TOP, 128), F32)], axis=0)

    def answer(coef_x, coef_a, centre):
        west, east = pltpu.roll(centre, 1, 0), pltpu.roll(centre, tall - 1, 0)
        south, north = roll_lanes(centre, 1), roll_lanes(centre, -1)
        return (
            centre + coef_x * (west - centre) + coef_a * (south - centre)
            + DIFFUSE * (west + east + south + north - 4.0 * centre)
        )

    coef_x, coef_a = tall_coef(0), tall_coef(1)
    first = RADIAL * theta
    second = jnp.where(valid, answer(coef_x, coef_a, first) + RADIAL * (theta - 2.0 * first), 0.0)
    second_126 = RADIAL * first
    third = answer(coef_x, coef_a, second) + RADIAL * (second_126 + theta - 2.0 * second)
    third_126 = answer(tall_only(courant[2]), tall_only(courant[3]), second_126) + RADIAL * (second - 2.0 * second_126)
    third_125 = RADIAL * second_126
    added = [flatten(value[TOP : TOP + rows], (1,))[0] for value in (third_125, third_126, third)]
    added = jnp.concatenate(added + [jnp.zeros((5, length), F32)], axis=0)
    added_high = added.astype(BF16).astype(F32)
    added = jnp.concatenate([added_high, added - added_high], axis=0).astype(BF16)
    radius = lax.broadcasted_iota(jnp.int32, (16, 128), 1) - 125
    which = lax.broadcasted_iota(jnp.int32, (16, 128), 0) % 8
    spread = jnp.where(jnp.logical_and(radius == which, which < 3), 1.0, 0.0).astype(BF16)
    added = lax.dot_general(added, spread, (((0,), (0,)), ((), ())), preferred_element_type=F32)
    gas_res[...] = gas_res[...] + added.reshape(rows, SECTOR, 128)

    wait_bytes(redbuf.at[1, pl.ds(0, nax - 1)], red_sem.at[3])
    sums = jnp.sum(redbuf[1, 0:nax], axis=0, keepdims=True)
    top = jnp.sum(jnp.where(lane1 == 0, sums, 0.0), axis=1, keepdims=True)
    bottom = jnp.sum(jnp.where(lane1 == 1, sums, 0.0), axis=1, keepdims=True)
    relax = -FIRST_RELAX * top / (bottom + TINY)
    th_res[...] = theta1 + relax * residual2

    wait_bytes(msg.at[pl.ds(0, naz - 1)], msg_sem.at[0])
    wait_bytes(msg.at[pl.ds(0, 2 * REACH), pl.ds(0, 32)], nb_sem.at[0])
    wait_bytes(th_rows.at[pl.ds(0, 8)], th_sem.at[0])
    wait_bytes(base_rows.at[pl.ds(0, 4)], base_sem.at[0])
    wait_bytes(edge.at[pl.ds(0, naz - 1)], edge_sem.at[0])

    @pl.when(at_rim)
    def _():
        wait_bytes(edge.at[pl.ds(0, naz)], edge_sem.at[2])

    wait_bytes(redbuf.at[0, pl.ds(0, naz - 1)], red_sem.at[0])
    wait_bytes(redbuf.at[1, pl.ds(0, nax - 1)], red_sem.at[2])


def write_out(gas_res, wall_res, th_res, gas_out, wall_out, th_out, sem):
    copies = [
        pltpu.make_async_copy(source, target, sem.at[index])
        for index, (source, target) in enumerate(((gas_res, gas_out), (wall_res, wall_out), (th_res, th_out)))
    ]
    for copy in copies:
        copy.start()
    for copy in copies:
        copy.wait()


def on_device(
    nax, naz, gas_init, transport, heat_coef, bed_mask, wall_init, interface_init, inverse_blocks, rotation
):
    rows = gas_init.shape[0]
    layers, length = wall_init.shape[1:]
    table_high, table_low = hartley_parts(length)
    anywhere = pl.BlockSpec(memory_space=pltpu.HBM)
    vmem = pl.BlockSpec(memory_space=pltpu.VMEM)
    dma = pltpu.SemaphoreType.DMA
    operands = [
        pltpu.with_memory_space_constraint(value, pltpu.HBM)
        for value in (
            gas_init, transport, heat_coef, bed_mask, wall_init.reshape(layers, length), interface_init,
            jnp.transpose(inverse_blocks, (1, 2, 0)),
            jnp.asarray(table_high), jnp.asarray(table_low), jnp.asarray(selector()),
        )
    ]
    gas_now, wall_now, theta = pl.pallas_call(
        functools.partial(kernel, nax, naz),
        out_shape=(
            jax.ShapeDtypeStruct(gas_init.shape, F32),
            jax.ShapeDtypeStruct((layers, length), F32),
            jax.ShapeDtypeStruct((1, length), F32),
        ),
        in_specs=[anywhere] * 7 + [pl.BlockSpec(memory_space=pltpu.SMEM)] + [anywhere] * 3,
        out_specs=(vmem,) * 3,
        scratch_shapes=[
            pltpu.VMEM((3, rows + 2, SECTOR + 2 * TOP, 128), F32),
            pltpu.VMEM(transport.shape, BF16),
            pltpu.VMEM(heat_coef.shape, F32),
            pltpu.VMEM(bed_mask.shape, jnp.int32),
            pltpu.VMEM((layers, length), F32),
            pltpu.VMEM((1, length), F32),
            pltpu.VMEM((layers, layers, length), F32),
            pltpu.VMEM((length, length), BF16),
            pltpu.VMEM((length, length), BF16),
            pltpu.VMEM((NFIELD, 5 * 128), BF16),
            pltpu.VMEM((rows, NFIELD, 128), BF16),
            pltpu.VMEM((naz, NFIELD, 128), BF16),
            pltpu.VMEM((naz, 32, 128), BF16),
            pltpu.VMEM((naz * NFIELD, 128), F32),
            pltpu.VMEM((16, length), F32),
            pltpu.VMEM((8, length), F32),
            pltpu.VMEM((naz, 128), F32),
            pltpu.VMEM((rows + 2 * TOP, 128), F32),
            pltpu.VMEM((2, rows, 128), F32),
            pltpu.VMEM((4, 2, rows, 128), F32),
            pltpu.VMEM((3, 2, rows, 128), F32),
            pltpu.VMEM((3, 2, rows, 128), F32),
            pltpu.VMEM((layers, length), F32),
            pltpu.VMEM((2, 128), F32),
            pltpu.VMEM((2, max(nax, naz), 128), F32),
            dma((10,)),
            dma((2,)),
            dma((2,)),
            dma((2,)),
            dma((2,)),
            dma((4,)),
            dma((3, 4)),
            dma((3, 4)),
            dma((4,)),
            dma((4,)),
            dma((4,)),
        ],
        compiler_params=pltpu.CompilerParams(
            collective_id=0, has_side_effects=True, vmem_limit_bytes=48 * 1024 * 1024
        ),
        name="kiln_step",
    )(
        *operands[:7], rotation, *operands[7:],
    )
    gas_now, wall_now, theta = pl.pallas_call(
        write_out,
        out_shape=[jax.ShapeDtypeStruct(value.shape, F32) for value in (gas_now, wall_now, theta)],
        in_specs=[vmem] * 3,
        out_specs=[anywhere] * 3,
        scratch_shapes=[dma((3,))],
        compiler_params=pltpu.CompilerParams(vmem_limit_bytes=1024 * 1024),
        name="write_out",
    )(gas_now, wall_now, theta)
    return gas_now, wall_now.reshape(1, layers, length), theta


def solution(mesh):
    return jax.shard_map(
        functools.partial(on_device, mesh.shape["ax"], mesh.shape["az"]),
        mesh=mesh,
        in_specs=(
            P("ax", "az", None),
            P(None, "ax", "az", None),
            P("ax", "az"),
            P("ax", "az"),
            P(("ax", "az"), None, None),
            P(("ax", "az"), None),
            P(),
            P(),
        ),
        out_specs=(P("ax", "az", None), P(("ax", "az"), None, None), P(("ax", "az"), None)),
        check_vma=False,
    )
```

time: 51.2 us -> 33.9 us (0.66)
  local copies, waits for them, and re-layouts: 12 us -> 0 us
  Pallas kernels: 37.4 us -> 32.5 us
    unnamed x23 -> x0, local copies, waits for them, and re-layouts: 12 us -> none
    pallas_call x1, Pallas kernels: 37.4 us -> 31.7 us  [on_device(): pl.pallas_call(functools.partial(kernel, nax, naz), out_shape=(jax.ShapeD...]
    pallas_call x0 -> x1, Pallas kernels: none -> 0.76 us  [on_device(): pl.pallas_call(write_out, out_shape=[jax.ShapeDtypeStruct(value.shape, F3...]
where the time goes in v1:
time: 33.9 us; the launch traced here: 33.8 us
  Pallas kernels  32.5 us (96%)
  between operations  1.29 us (4%)
    pallas_call x1, Pallas kernels, on_device(): pl.pallas_call(functools.partial(kernel, nax, naz), out_shape=(jax.ShapeD...  31.7 us
    pallas_call x1, Pallas kernels, on_device(): pl.pallas_call(write_out, out_shape=[jax.ShapeDtypeStruct(value.shape, F3...  0.76 us

profile of v1, /device:TPU:1, one launch (start us, length us, event | category | flops | bytes accessed | tf_op | source)
XLA Modules:
  0.0 33.8 jit_solution(8527499947438546498)
XLA Ops:
  1.3 31.7 %kiln_step.1 = (f32[16,32,128]{2,1,0:T(8,128)S(1)}, f32[48,512]{1,0:T(8,128)S(1)}, f32[1,512]{1,0:T(1,128)S(1)}) custom-call(f32[16,32,128]{2,1,0:T(8,128)} %gas_hbm.1, bf16[3,16,32,128]{3,2,1,0:T(8,128)(2,1)} %tr_hbm.1, f32[16,32]{1,0:T(8,128)} %heat_hbm.1, s32[16,32]{1,0:T(8,128)} %bed_hbm.1, f32[48,512]{1,0:T(8,128)} %bitcast.4, f32[1,512]{1,0:T(1,128)} %th_hbm.1, ...), custom_call_target="tpu_custom_call" | custom-call | tf_op jit(solution)/shard_map/kiln_step/pallas_call | solution.py:650
  33.0 0.8 %write_out.1 = (f32[16,32,128]{2,1,0:T(8,128)}, f32[48,512]{1,0:T(8,128)}, f32[1,512]{1,0:T(1,128)}) custom-call(f32[16,32,128]{2,1,0:T(8,128)S(1)} %get-tuple-element.9.gas_res, f32[48,512]{1,0:T(8,128)S(1)} %get-tuple-element.10.wall_res, f32[1,512]{1,0:T(1,128)S(1)} %get-tuple-element.11.th_res), custom_call_target="tpu_custom_call" | custom-call | tf_op jit(solution)/shard_map/write_out/pallas_call | solution.py:704

commit v2 on v1

--- a/solution.py
+++ b/solution.py
@@ -217,17 +217,6 @@
     def wait_bytes(ref, sem):
         pltpu.make_async_copy(ref, ref, sem).wait()
 
-    @pl.loop(0, REACH)
-    def _(k):
-        remote(msg.at[k, pl.ds(0, 32)], recv_nb.at[az], nb_sem.at[0], nb_sem.at[1], up_ax, k).start()
-        high = naz - REACH + k
-        remote(msg.at[high, pl.ds(16, 32)], recv_nb.at[az], nb_sem.at[0], nb_sem.at[1], down_ax, high).start()
-
-    @pl.loop(1, naz)
-    def _(k):
-        to = lax.rem(az + k, naz)
-        remote(msg.at[to], recv.at[az], msg_sem.at[0], msg_sem.at[1], ax, to).start()
-
     def send_row(ref, slot, reach, sems):
         for offset in range(-reach, reach + 1):
             if offset:
@@ -238,32 +227,6 @@
                 ).start()
 
     send_row(th_rows, 4, 4, th_sem)
-
-    def times_table(value):
-        high, low = split(value)
-        count = value.shape[0]
-        both = jnp.dot(jnp.concatenate([high, low], axis=0), hh[...], preferred_element_type=F32)
-        return both[:count] + both[count:] + jnp.dot(high, hl[...], preferred_element_type=F32)
-
-    def rows_times_table(value):
-        count = value.shape[0]
-        value = jnp.concatenate([value, jnp.zeros((8 - count, length), F32)], axis=0)
-        high = value.astype(BF16).astype(F32)
-        both = jnp.concatenate([high, value - high], axis=0).astype(BF16)
-        first = jnp.dot(both, hh[...], preferred_element_type=F32)
-        second = jnp.dot(both, hl[...], preferred_element_type=F32)
-        return (first[0:8] + first[8:16] + second[0:8])[:count]
-
-    loads["wall"].wait()
-    loads["hh"].wait()
-    loads["hl"].wait()
-    layers = wall.shape[0]
-    spectral = times_table(wall[...])
-    loads["inv"].wait()
-    mode_gain = inv[0, 0:1, :]
-    mode_base = jnp.sum(inv[0] * spectral, axis=0, keepdims=True)
-    base_rows[2:3, :] = mode_base
-    send_row(base_rows, 2, 2, base_sem)
 
     def halo_copies(step):
         return (
@@ -281,6 +244,45 @@
         for copy in halo_copies(step):
             copy.start()
 
+    send_halo(0)
+
+    @pl.loop(0, REACH)
+    def _(k):
+        remote(msg.at[k, pl.ds(0, 32)], recv_nb.at[az], nb_sem.at[0], nb_sem.at[1], up_ax, k).start()
+        high = naz - REACH + k
+        remote(msg.at[high, pl.ds(16, 32)], recv_nb.at[az], nb_sem.at[0], nb_sem.at[1], down_ax, high).start()
+
+    @pl.loop(1, naz)
+    def _(k):
+        to = lax.rem(az + k, naz)
+        remote(msg.at[to], recv.at[az], msg_sem.at[0], msg_sem.at[1], ax, to).start()
+
+    def times_table(value):
+        high, low = split(value)
+        count = value.shape[0]
+        both = jnp.dot(jnp.concatenate([high, low], axis=0), hh[...], preferred_element_type=F32)
+        return both[:count] + both[count:] + jnp.dot(high, hl[...], preferred_element_type=F32)
+
+    def rows_times_table(value):
+        count = value.shape[0]
+        value = jnp.concatenate([value, jnp.zeros((8 - count, length), F32)], axis=0)
+        high = value.astype(BF16).astype(F32)
+        both = jnp.concatenate([high, value - high], axis=0).astype(BF16)
+        first = jnp.dot(both, hh[...], preferred_element_type=F32)
+        second = jnp.dot(both, hl[...], preferred_element_type=F32)
+        return (first[0:8] + first[8:16] + second[0:8])[:count]
+
+    loads["wall"].wait()
+    loads["hh"].wait()
+    loads["hl"].wait()
+    layers = wall.shape[0]
+    spectral = times_table(wall[...])
+    loads["inv"].wait()
+    mode_gain = inv[0, 0:1, :]
+    mode_base = jnp.sum(inv[0] * spectral, axis=0, keepdims=True)
+    base_rows[2:3, :] = mode_base
+    send_row(base_rows, 2, 2, base_sem)
+
     def take_halo(step):
         for copy in halo_copies(step):
             copy.wait()
@@ -296,7 +298,6 @@
         pad[step, 1 : rows + 1, TOP - 1, :] = col_in[step, 0]
         pad[step, 1 : rows + 1, TOP + SECTOR, :] = col_in[step, 1]
 
-    send_halo(0)
     coef_copies = [
         remote(coef_out, coef_in.at[slot], coef_ss.at[slot], coef_rs.at[slot], to_ax, to_az)
         for slot, (to_ax, to_az) in enumerate(((up_ax, az), (down_ax, az), (ax, up_az), (ax, down_az)))
@@ -344,7 +345,7 @@
 
     wait_bytes(recv.at[pl.ds(0, naz - 1)], msg_sem.at[1])
 
-    @pl.loop(0, naz)
+    @pl.loop(0, naz, unroll=True)
     def _(source):
         fields[pl.ds(pl.multiple_of(source * NFIELD, NFIELD), NFIELD), :] = recv[source].astype(F32)
 
@@ -357,7 +358,7 @@
         place = az + firsts + lax.broadcasted_iota(jnp.int32, (32, 128), 1) // SECTOR
         own = jnp.logical_and(place >= 0, place < rows)
 
-        @pl.loop(0, naz)
+        @pl.loop(0, naz, unroll=4)
         def _(source):
             here = pl.ds(pl.multiple_of(source * NFIELD + start, 16), 32)
             fields[here, :] = jnp.where(own, fields[here, :], recv_nb[source].astype(F32))

time: 33.9 us -> 32.4 us (0.956)
  Pallas kernels: 32.5 us -> 31 us
    pallas_call x1, Pallas kernels: 31.7 us -> 30.3 us  [on_device(): pl.pallas_call(functools.partial(kernel, nax, naz), out_shape=(jax.ShapeD...]
where the time goes in v2:
time: 32.4 us; the launch traced here: 32.3 us
  Pallas kernels  31 us (96%)
  between operations  1.29 us (4%)
    pallas_call x1, Pallas kernels, on_device(): pl.pallas_call(functools.partial(kernel, nax, naz), out_shape=(jax.ShapeD...  30.3 us
    pallas_call x1, Pallas kernels, on_device(): pl.pallas_call(write_out, out_shape=[jax.ShapeDtypeStruct(value.shape, F3...  0.76 us

profile of v2, /device:TPU:1, one launch (start us, length us, event | category | flops | bytes accessed | tf_op | source)
XLA Modules:
  0.0 32.3 jit_solution(17669495168042603473)
XLA Ops:
  1.3 30.3 %kiln_step.1 = (f32[16,32,128]{2,1,0:T(8,128)S(1)}, f32[48,512]{1,0:T(8,128)S(1)}, f32[1,512]{1,0:T(1,128)S(1)}) custom-call(f32[16,32,128]{2,1,0:T(8,128)} %gas_hbm.1, bf16[3,16,32,128]{3,2,1,0:T(8,128)(2,1)} %tr_hbm.1, f32[16,32]{1,0:T(8,128)} %heat_hbm.1, s32[16,32]{1,0:T(8,128)} %bed_hbm.1, f32[48,512]{1,0:T(8,128)} %bitcast.4, f32[1,512]{1,0:T(1,128)} %th_hbm.1, ...), custom_call_target="tpu_custom_call" | custom-call | tf_op jit(solution)/shard_map/kiln_step/pallas_call | solution.py:651
  31.6 0.8 %write_out.1 = (f32[16,32,128]{2,1,0:T(8,128)}, f32[48,512]{1,0:T(8,128)}, f32[1,512]{1,0:T(1,128)}) custom-call(f32[16,32,128]{2,1,0:T(8,128)S(1)} %get-tuple-element.9.gas_res, f32[48,512]{1,0:T(8,128)S(1)} %get-tuple-element.10.wall_res, f32[1,512]{1,0:T(1,128)S(1)} %get-tuple-element.11.th_res), custom_call_target="tpu_custom_call" | custom-call | tf_op jit(solution)/shard_map/write_out/pallas_call | solution.py:705

commit v3 on v2

--- a/solution.py
+++ b/solution.py
@@ -81,6 +81,32 @@
     up_az, down_az = lax.rem(az + 1, naz), lax.rem(az + naz - 1, naz)
     inside = pl.ds(TOP, SECTOR)
 
+    barrier = pltpu.get_barrier_semaphore()
+
+    def greet(to_ax, to_az):
+        pl.semaphore_signal(barrier, inc=1, device_id=(to_ax, to_az), device_id_type=MESH)
+
+    low_edge, high_edge = az < REACH, az >= naz - REACH
+    at_edge = jnp.logical_or(low_edge, high_edge)
+    beside = jnp.where(low_edge, down_ax, up_ax)
+    at_rim = jnp.logical_or(az < 2, az >= naz - 2)
+
+    @pl.when(at_edge)
+    def _():
+        @pl.loop(0, naz)
+        def _(k):
+            greet(beside, k)
+
+    for k in range(2):
+        greet(up_ax, k)
+        greet(down_ax, naz - 2 + k)
+
+    for k in sorted(range(1, max(nax, naz)), key=lambda k: -min(k, max(nax, naz) - k)):
+        if k < nax:
+            greet(lax.rem(ax + k, nax), az)
+        if k < naz:
+            greet(ax, lax.rem(az + k, naz))
+
     loads = {}
     for index, (name, source, target) in enumerate((
         ("gas", gas_hbm, pad.at[0, pl.ds(1, rows), inside]),
@@ -96,34 +122,6 @@
     )):
         loads[name] = pltpu.make_async_copy(source, target, load_sem.at[index])
         loads[name].start()
-
-    barrier = pltpu.get_barrier_semaphore()
-
-    def greet(to_ax, to_az):
-        pl.semaphore_signal(barrier, inc=1, device_id=(to_ax, to_az), device_id_type=MESH)
-
-    @pl.loop(1, naz)
-    def _(k):
-        greet(ax, lax.rem(az + k, naz))
-
-    @pl.loop(1, nax)
-    def _(k):
-        greet(lax.rem(ax + k, nax), az)
-
-    low_edge, high_edge = az < REACH, az >= naz - REACH
-    at_edge = jnp.logical_or(low_edge, high_edge)
-    beside = jnp.where(low_edge, down_ax, up_ax)
-    at_rim = jnp.logical_or(az < 2, az >= naz - 2)
-
-    @pl.when(at_edge)
-    def _():
-        @pl.loop(0, naz)
-        def _(k):
-            greet(beside, k)
-
-    for k in range(2):
-        greet(up_ax, k)
-        greet(down_ax, naz - 2 + k)
 
     lane = lax.broadcasted_iota(jnp.int32, (naz, 128), 1)
     sector = lax.broadcasted_iota(jnp.int32, (naz, 128), 0)
@@ -217,6 +215,11 @@
     def wait_bytes(ref, sem):
         pltpu.make_async_copy(ref, ref, sem).wait()
 
+    def edge_part(row):
+        if row < REACH:
+            return pl.ds(0, 32 if row < 2 else 16)
+        return pl.ds(16, 32) if row > naz - REACH else pl.ds(32, 16)
+
     def send_row(ref, slot, reach, sems):
         for offset in range(-reach, reach + 1):
             if offset:
@@ -246,16 +249,18 @@
 
     send_halo(0)
 
-    @pl.loop(0, REACH)
-    def _(k):
-        remote(msg.at[k, pl.ds(0, 32)], recv_nb.at[az], nb_sem.at[0], nb_sem.at[1], up_ax, k).start()
-        high = naz - REACH + k
-        remote(msg.at[high, pl.ds(16, 32)], recv_nb.at[az], nb_sem.at[0], nb_sem.at[1], down_ax, high).start()
-
-    @pl.loop(1, naz)
-    def _(k):
+    for k in sorted(range(1, naz), key=lambda k: -min(k // 4, 4 - k // 4) - min(k % 4, 4 - k % 4)):
         to = lax.rem(az + k, naz)
         remote(msg.at[to], recv.at[az], msg_sem.at[0], msg_sem.at[1], ax, to).start()
+
+    for k in range(REACH):
+        part = edge_part(k)
+        remote(msg.at[k, part], recv_nb.at[az, pl.ds(0, part.size)], nb_sem.at[0], nb_sem.at[1], up_ax, k).start()
+        high = naz - REACH + k
+        part = edge_part(high)
+        remote(
+            msg.at[high, part], recv_nb.at[az, pl.ds(0, part.size)], nb_sem.at[0], nb_sem.at[1], down_ax, high
+        ).start()
 
     def times_table(value):
         high, low = split(value)
@@ -315,7 +320,7 @@
     lane_row = lax.broadcasted_iota(jnp.int32, (SECTOR, 128), 1)
 
     def sweep(step, store):
-        @pl.loop(0, rows)
+        @pl.loop(0, rows, unroll=2)
         def _(x):
             centre = pad[step, x + 1, inside, :]
             west = pad[step, x, inside, :]
@@ -338,6 +343,11 @@
             pad[step, x + 1, inside, :] = value
         return store
 
+    wait_bytes(th_rows.at[pl.ds(0, 8)], th_sem.at[1])
+    start = th_rows[0:9, :]
+    rows_of = lambda values, *picks: tile_rows([None if k is None else values[k : k + 1] for k in picks])
+    start_edges = [rows_of(start, 0, 1, 2, 3), rows_of(start, 4, 5, 6, 7), rows_of(start, 8, None, None, None)]
+
     take_halo(0)
     sweep(0, store_pad(1))
     stage_columns(1)
@@ -349,29 +359,29 @@
     def _(source):
         fields[pl.ds(pl.multiple_of(source * NFIELD, NFIELD), NFIELD), :] = recv[source].astype(F32)
 
-    def merge(start):
-        firsts = jnp.zeros((32, 128), jnp.int32)
-        index = lax.broadcasted_iota(jnp.int32, (32, 128), 0)
-        for j in range(32):
+    def merge(start, count):
+        wait_bytes(recv_nb.at[pl.ds(0, naz), pl.ds(0, count)], nb_sem.at[1])
+        firsts = jnp.zeros((count, 128), jnp.int32)
+        index = lax.broadcasted_iota(jnp.int32, (count, 128), 0)
+        for j in range(count):
             if j == 0 or FIRSTS[start + j] != FIRSTS[start + j - 1]:
                 firsts = jnp.where(index >= j, FIRSTS[start + j], firsts)
-        place = az + firsts + lax.broadcasted_iota(jnp.int32, (32, 128), 1) // SECTOR
+        place = az + firsts + lax.broadcasted_iota(jnp.int32, (count, 128), 1) // SECTOR
         own = jnp.logical_and(place >= 0, place < rows)
 
         @pl.loop(0, naz, unroll=4)
         def _(source):
-            here = pl.ds(pl.multiple_of(source * NFIELD + start, 16), 32)
-            fields[here, :] = jnp.where(own, fields[here, :], recv_nb[source].astype(F32))
-
-    @pl.when(low_edge)
-    def _():
-        wait_bytes(recv_nb, nb_sem.at[1])
-        merge(0)
-
-    @pl.when(high_edge)
-    def _():
-        wait_bytes(recv_nb, nb_sem.at[1])
-        merge(16)
+            here = pl.ds(pl.multiple_of(source * NFIELD + start, 16), count)
+            fields[here, :] = jnp.where(own, fields[here, :], recv_nb[source, 0:count].astype(F32))
+
+    for chosen, row in (
+        (az < 2, 0),
+        (jnp.logical_and(az >= 2, low_edge), 2),
+        (az == naz - REACH, naz - REACH),
+        (az > naz - REACH, naz - 1),
+    ):
+        part = edge_part(row)
+        pl.when(chosen)(functools.partial(merge, part.start, part.size))
 
     def field(index):
         return fields[pl.ds(index, naz, stride=NFIELD), :]
@@ -474,12 +484,7 @@
         face = rows_times_table(modes * mode_gain + without)
         return modes, pltpu.roll(face, shift, 1)
 
-    wait_bytes(th_rows.at[pl.ds(0, 8)], th_sem.at[1])
-    start = th_rows[0:9, :]
-    rows_of = lambda values, *picks: tile_rows([None if k is None else values[k : k + 1] for k in picks])
-    flux = near_flux(
-        [rows_of(start, 0, 1, 2, 3), rows_of(start, 4, 5, 6, 7), rows_of(start, 8, None, None, None)], (0, 1)
-    )
+    flux = near_flux(start_edges, (0, 1))
     flux = jnp.concatenate(flatten(flux[0], (2, 3)) + flatten(flux[1], (0, 1, 2)), axis=0)
     wait_bytes(base_rows.at[pl.ds(0, 4)], base_sem.at[1])
     _, face = wall_face(flux, base_rows[0:5, :])
@@ -607,7 +612,7 @@
     th_res[...] = theta1 + relax * residual2
 
     wait_bytes(msg.at[pl.ds(0, naz - 1)], msg_sem.at[0])
-    wait_bytes(msg.at[pl.ds(0, 2 * REACH), pl.ds(0, 32)], nb_sem.at[0])
+    wait_bytes(msg.at[pl.ds(0, 8), pl.ds(0, 32)], nb_sem.at[0])
     wait_bytes(th_rows.at[pl.ds(0, 8)], th_sem.at[0])
     wait_bytes(base_rows.at[pl.ds(0, 4)], base_sem.at[0])
     wait_bytes(edge.at[pl.ds(0, naz - 1)], edge_sem.at[0])

time: 32.4 us -> 31.4 us (0.969)
  Pallas kernels: 31 us -> 30 us
    pallas_call x1, Pallas kernels: 30.3 us -> 29.3 us  [on_device(): pl.pallas_call(functools.partial(kernel, nax, naz), out_shape=(jax.ShapeD...]
where the time goes in v3:
time: 31.4 us; the launch traced here: 31.3 us
  Pallas kernels  30 us (96%)
  between operations  1.29 us (4%)
    pallas_call x1, Pallas kernels, on_device(): pl.pallas_call(functools.partial(kernel, nax, naz), out_shape=(jax.ShapeD...  29.3 us
    pallas_call x1, Pallas kernels, on_device(): pl.pallas_call(write_out, out_shape=[jax.ShapeDtypeStruct(value.shape, F3...  0.76 us

profile of v3, /device:TPU:1, one launch (start us, length us, event | category | flops | bytes accessed | tf_op | source)
XLA Modules:
  0.0 31.3 jit_solution(16311162702856573722)
XLA Ops:
  1.3 29.3 %kiln_step.1 = (f32[16,32,128]{2,1,0:T(8,128)S(1)}, f32[48,512]{1,0:T(8,128)S(1)}, f32[1,512]{1,0:T(1,128)S(1)}) custom-call(f32[16,32,128]{2,1,0:T(8,128)} %gas_hbm.1, bf16[3,16,32,128]{3,2,1,0:T(8,128)(2,1)} %tr_hbm.1, f32[16,32]{1,0:T(8,128)} %heat_hbm.1, s32[16,32]{1,0:T(8,128)} %bed_hbm.1, f32[48,512]{1,0:T(8,128)} %bitcast.4, f32[1,512]{1,0:T(1,128)} %th_hbm.1, ...), custom_call_target="tpu_custom_call" | custom-call | tf_op jit(solution)/shard_map/kiln_step/pallas_call | solution.py:656
  30.5 0.8 %write_out.1 = (f32[16,32,128]{2,1,0:T(8,128)}, f32[48,512]{1,0:T(8,128)}, f32[1,512]{1,0:T(1,128)}) custom-call(f32[16,32,128]{2,1,0:T(8,128)S(1)} %get-tuple-element.9.gas_res, f32[48,512]{1,0:T(8,128)S(1)} %get-tuple-element.10.wall_res, f32[1,512]{1,0:T(1,128)S(1)} %get-tuple-element.11.th_res), custom_call_target="tpu_custom_call" | custom-call | tf_op jit(solution)/shard_map/write_out/pallas_call | solution.py:710

commit v4 on v3

--- a/solution.py
+++ b/solution.py
@@ -66,7 +66,7 @@
     nax, naz,
     gas_hbm, tr_hbm, heat_hbm, bed_hbm, wall_hbm, th_hbm, inv_hbm, rot_ref, hh_hbm, hl_hbm, sel_hbm,
     gas_res, wall_res, th_res,
-    pad, tr, heat, bed, wall, th, inv, hh, hl, sel,
+    pad, tr, heat, bed, wall, th, inv, hh, hl, gh, gl, sel,
     msg, recv, recv_nb, fields, th_rows, base_rows, window, edge, coef_out, coef_in, col_out, col_in, blend,
     redsrc, redbuf,
     load_sem, msg_sem, nb_sem, th_sem, base_sem, edge_sem, halo_ss, halo_rs, coef_ss, coef_rs, red_sem,
@@ -268,13 +268,13 @@
         both = jnp.dot(jnp.concatenate([high, low], axis=0), hh[...], preferred_element_type=F32)
         return both[:count] + both[count:] + jnp.dot(high, hl[...], preferred_element_type=F32)
 
-    def rows_times_table(value):
+    def rows_times_table(value, high_table=hh, low_table=hl):
         count = value.shape[0]
         value = jnp.concatenate([value, jnp.zeros((8 - count, length), F32)], axis=0)
         high = value.astype(BF16).astype(F32)
         both = jnp.concatenate([high, value - high], axis=0).astype(BF16)
-        first = jnp.dot(both, hh[...], preferred_element_type=F32)
-        second = jnp.dot(both, hl[...], preferred_element_type=F32)
+        first = jnp.dot(both, high_table[...], preferred_element_type=F32)
+        second = jnp.dot(both, low_table[...], preferred_element_type=F32)
         return (first[0:8] + first[8:16] + second[0:8])[:count]
 
     loads["wall"].wait()
@@ -285,7 +285,7 @@
     loads["inv"].wait()
     mode_gain = inv[0, 0:1, :]
     mode_base = jnp.sum(inv[0] * spectral, axis=0, keepdims=True)
-    base_rows[2:3, :] = mode_base
+    base_rows[2:3, :] = rows_times_table(mode_base)
     send_row(base_rows, 2, 2, base_sem)
 
     def take_halo(step):
@@ -307,8 +307,6 @@
         remote(coef_out, coef_in.at[slot], coef_ss.at[slot], coef_rs.at[slot], to_ax, to_az)
         for slot, (to_ax, to_az) in enumerate(((up_ax, az), (down_ax, az), (ax, up_az), (ax, down_az)))
     ]
-    for copy in coef_copies:
-        copy.start()
     recv[az] = msg[az]
 
     @pl.loop(0, layers // 2)
@@ -316,6 +314,14 @@
         for j in range(2):
             layer = 2 * pair + j
             blend[pl.ds(layer, 1), :] = jnp.sum(inv[layer] * spectral, axis=0, keepdims=True)
+
+    scaled_high, scaled_low = split((hh[...].astype(F32) + hl[...].astype(F32)) * mode_gain)
+    both = (
+        jnp.dot(scaled_high, hh[...], preferred_element_type=F32)
+        + jnp.dot(scaled_low, hh[...], preferred_element_type=F32)
+        + jnp.dot(scaled_high, hl[...], preferred_element_type=F32)
+    )
+    gh[...], gl[...] = split(both)
 
     lane_row = lax.broadcasted_iota(jnp.int32, (SECTOR, 128), 1)
 
@@ -480,9 +486,9 @@
     shift_back = length - shift
 
     def wall_face(flux, without):
-        modes = rows_times_table(pltpu.roll(flux, shift_back, 1))
-        face = rows_times_table(modes * mode_gain + without)
-        return modes, pltpu.roll(face, shift, 1)
+        turned_flux = pltpu.roll(flux, shift_back, 1)
+        face = rows_times_table(turned_flux, gh, gl) + without
+        return turned_flux, pltpu.roll(face, shift, 1)
 
     flux = near_flux(start_edges, (0, 1))
     flux = jnp.concatenate(flatten(flux[0], (2, 3)) + flatten(flux[1], (0, 1, 2)), axis=0)
@@ -493,7 +499,7 @@
     flux = near_flux(
         [rows_of(theta1, None, None, 0, 1), rows_of(theta1, 2, 3, 4, None), none], (1,)
     )
-    modes, face = wall_face(flatten(flux[0], (0,))[0], mode_base)
+    turned_flux, face = wall_face(flatten(flux[0], (0,))[0], base_rows[2:3, :])
     residual1 = residual1[2:3]
     theta1 = theta1[2:3]
     residual2 = face - theta1
@@ -535,7 +541,10 @@
 
     edge[pl.ds(TOP + az, 1), :] = window[pl.ds(az, 1), :]
 
-    wall_res[...] = times_table(blend[...] + inv[:, 0, :] * modes)
+    for copy in coef_copies:
+        copy.start()
+
+    wall_res[...] = times_table(blend[...] + inv[:, 0, :] * rows_times_table(turned_flux))
 
     take_halo(1)
     sweep(1, store_pad(2))
@@ -670,6 +679,8 @@
             pltpu.VMEM((layers, length), F32),
             pltpu.VMEM((1, length), F32),
             pltpu.VMEM((layers, layers, length), F32),
+            pltpu.VMEM((length, length), BF16),
+            pltpu.VMEM((length, length), BF16),
             pltpu.VMEM((length, length), BF16),
             pltpu.VMEM((length, length), BF16),
             pltpu.VMEM((NFIELD, 5 * 128), BF16),

time: 31.4 us -> 30.9 us (0.984)
  Pallas kernels: 30 us -> 29.5 us
    pallas_call x1, Pallas kernels: 29.3 us -> 28.7 us  [on_device(): pl.pallas_call(functools.partial(kernel, nax, naz), out_shape=(jax.ShapeD...]
where the time goes in v4:
time: 30.9 us; the launch traced here: 30.8 us
  Pallas kernels  29.5 us (95%)
  between operations  1.29 us (4%)
    pallas_call x1, Pallas kernels, on_device(): pl.pallas_call(functools.partial(kernel, nax, naz), out_shape=(jax.ShapeD...  28.7 us
    pallas_call x1, Pallas kernels, on_device(): pl.pallas_call(write_out, out_shape=[jax.ShapeDtypeStruct(value.shape, F3...  0.76 us

profile of v4, /device:TPU:1, one launch (start us, length us, event | category | flops | bytes accessed | tf_op | source)
XLA Modules:
  0.0 30.8 jit_solution(6627672337976853970)
XLA Ops:
  1.3 28.7 %kiln_step.1 = (f32[16,32,128]{2,1,0:T(8,128)S(1)}, f32[48,512]{1,0:T(8,128)S(1)}, f32[1,512]{1,0:T(1,128)S(1)}) custom-call(f32[16,32,128]{2,1,0:T(8,128)} %gas_hbm.1, bf16[3,16,32,128]{3,2,1,0:T(8,128)(2,1)} %tr_hbm.1, f32[16,32]{1,0:T(8,128)} %heat_hbm.1, s32[16,32]{1,0:T(8,128)} %bed_hbm.1, f32[48,512]{1,0:T(8,128)} %bitcast.4, f32[1,512]{1,0:T(1,128)} %th_hbm.1, ...), custom_call_target="tpu_custom_call" | custom-call | tf_op jit(solution)/shard_map/kiln_step/pallas_call | solution.py:665
  30.0 0.8 %write_out.1 = (f32[16,32,128]{2,1,0:T(8,128)}, f32[48,512]{1,0:T(8,128)}, f32[1,512]{1,0:T(1,128)}) custom-call(f32[16,32,128]{2,1,0:T(8,128)S(1)} %get-tuple-element.9.gas_res, f32[48,512]{1,0:T(8,128)S(1)} %get-tuple-element.10.wall_res, f32[1,512]{1,0:T(1,128)S(1)} %get-tuple-element.11.th_res), custom_call_target="tpu_custom_call" | custom-call | tf_op jit(solution)/shard_map/write_out/pallas_call | solution.py:721

commit v5 on v4

--- a/solution.py
+++ b/solution.py
@@ -67,7 +67,7 @@
     gas_hbm, tr_hbm, heat_hbm, bed_hbm, wall_hbm, th_hbm, inv_hbm, rot_ref, hh_hbm, hl_hbm, sel_hbm,
     gas_res, wall_res, th_res,
     pad, tr, heat, bed, wall, th, inv, hh, hl, gh, gl, sel,
-    msg, recv, recv_nb, fields, th_rows, base_rows, window, edge, coef_out, coef_in, col_out, col_in, blend,
+    msg, recv, recv_nb, fields, th_rows, base_rows, window, edge, coef_out, coef_in, col_out, col_in, row_in, blend,
     redsrc, redbuf,
     load_sem, msg_sem, nb_sem, th_sem, base_sem, edge_sem, halo_ss, halo_rs, coef_ss, coef_rs, red_sem,
 ):
@@ -233,9 +233,9 @@
 
     def halo_copies(step):
         return (
-            remote(pad.at[step, rows, inside], pad.at[step, 0, inside],
+            remote(pad.at[step, rows, inside], pad.at[step, 0, inside] if step else row_in.at[0],
                    halo_ss.at[step, 0], halo_rs.at[step, 0], up_ax, az),
-            remote(pad.at[step, 1, inside], pad.at[step, rows + 1, inside],
+            remote(pad.at[step, 1, inside], pad.at[step, rows + 1, inside] if step else row_in.at[1],
                    halo_ss.at[step, 1], halo_rs.at[step, 1], down_ax, az),
             remote(col_out.at[step, 1], col_in.at[step, 0],
                    halo_ss.at[step, 2], halo_rs.at[step, 2], ax, up_az),
@@ -308,12 +308,6 @@
         for slot, (to_ax, to_az) in enumerate(((up_ax, az), (down_ax, az), (ax, up_az), (ax, down_az)))
     ]
     recv[az] = msg[az]
-
-    @pl.loop(0, layers // 2)
-    def _(pair):
-        for j in range(2):
-            layer = 2 * pair + j
-            blend[pl.ds(layer, 1), :] = jnp.sum(inv[layer] * spectral, axis=0, keepdims=True)
 
     scaled_high, scaled_low = split((hh[...].astype(F32) + hl[...].astype(F32)) * mode_gain)
     both = (
@@ -354,8 +348,20 @@
     rows_of = lambda values, *picks: tile_rows([None if k is None else values[k : k + 1] for k in picks])
     start_edges = [rows_of(start, 0, 1, 2, 3), rows_of(start, 4, 5, 6, 7), rows_of(start, 8, None, None, None)]
 
-    take_halo(0)
+    for edge_row in (0, rows + 1):
+        pad[0, edge_row, inside, :] = jnp.zeros((SECTOR, 128), F32)
+    for edge_column in (TOP - 1, TOP + SECTOR):
+        pad[0, 1 : rows + 1, edge_column, :] = jnp.zeros((rows, 128), F32)
     sweep(0, store_pad(1))
+    swirl = tr[1, :, 0:16, :].astype(F32)[:, 0, :]
+    for copy in halo_copies(0):
+        copy.wait()
+    west = jnp.where(ax > 0, row_in[0], 0.0)
+    east = jnp.where(ax < nax - 1, row_in[1], 0.0)
+    pad[1, 1, inside, :] = pad[1, 1, inside, :] + (tr[0, 0].astype(F32) + DIFFUSE) * west
+    pad[1, rows, inside, :] = pad[1, rows, inside, :] + DIFFUSE * east
+    pad[1, 1 : rows + 1, TOP, :] = pad[1, 1 : rows + 1, TOP, :] + (swirl + DIFFUSE) * col_in[0, 0]
+    pad[1, 1 : rows + 1, TOP + SECTOR - 1, :] = pad[1, 1 : rows + 1, TOP + SECTOR - 1, :] + DIFFUSE * col_in[0, 1]
     stage_columns(1)
     send_halo(1)
 
@@ -543,6 +549,12 @@
 
     for copy in coef_copies:
         copy.start()
+
+    @pl.loop(0, layers // 2)
+    def _(pair):
+        for j in range(2):
+            layer = 2 * pair + j
+            blend[pl.ds(layer, 1), :] = jnp.sum(inv[layer] * spectral, axis=0, keepdims=True)
 
     wall_res[...] = times_table(blend[...] + inv[:, 0, :] * rows_times_table(turned_flux))
 
@@ -696,6 +708,7 @@
             pltpu.VMEM((4, 2, rows, 128), F32),
             pltpu.VMEM((3, 2, rows, 128), F32),
             pltpu.VMEM((3, 2, rows, 128), F32),
+            pltpu.VMEM((2, SECTOR, 128), F32),
             pltpu.VMEM((layers, length), F32),
             pltpu.VMEM((2, 128), F32),
             pltpu.VMEM((2, max(nax, naz), 128), F32),

time: 30.9 us -> 30.9 us (level)
  no operation moved by 1% of the time
where the time goes in v5:
time: 30.9 us; the launch traced here: 30.8 us
  Pallas kernels  29.5 us (95%)
  between operations  1.29 us (4%)
    pallas_call x1, Pallas kernels, on_device(): pl.pallas_call(functools.partial(kernel, nax, naz), out_shape=(jax.ShapeD...  28.7 us
    pallas_call x1, Pallas kernels, on_device(): pl.pallas_call(write_out, out_shape=[jax.ShapeDtypeStruct(value.shape, F3...  0.76 us

profile of v5, /device:TPU:1, one launch (start us, length us, event | category | flops | bytes accessed | tf_op | source)
XLA Modules:
  0.0 30.8 jit_solution(10998789010095742967)
XLA Ops:
  1.3 28.7 %kiln_step.1 = (f32[16,32,128]{2,1,0:T(8,128)S(1)}, f32[48,512]{1,0:T(8,128)S(1)}, f32[1,512]{1,0:T(1,128)S(1)}) custom-call(f32[16,32,128]{2,1,0:T(8,128)} %gas_hbm.1, bf16[3,16,32,128]{3,2,1,0:T(8,128)(2,1)} %tr_hbm.1, f32[16,32]{1,0:T(8,128)} %heat_hbm.1, s32[16,32]{1,0:T(8,128)} %bed_hbm.1, f32[48,512]{1,0:T(8,128)} %bitcast.4, f32[1,512]{1,0:T(1,128)} %th_hbm.1, ...), custom_call_target="tpu_custom_call" | custom-call | tf_op jit(solution)/shard_map/kiln_step/pallas_call | solution.py:677
  30.0 0.8 %write_out.1 = (f32[16,32,128]{2,1,0:T(8,128)}, f32[48,512]{1,0:T(8,128)}, f32[1,512]{1,0:T(1,128)}) custom-call(f32[16,32,128]{2,1,0:T(8,128)S(1)} %get-tuple-element.9.gas_res, f32[48,512]{1,0:T(8,128)S(1)} %get-tuple-element.10.wall_res, f32[1,512]{1,0:T(1,128)S(1)} %get-tuple-element.11.th_res), custom_call_target="tpu_custom_call" | custom-call | tf_op jit(solution)/shard_map/write_out/pallas_call | solution.py:734
